TPU v7x, 32 devices: a whole 2x2x4 slice. The times are simulated.
32 devices in a mesh: dp: 8 (over y, x, core), tensor: 4 (over z).
Axes of the slice: x: 2, y: 2, z: 4, core: 2. Of those that a mesh axis runs over, the one named last changes fastest.
Arguments:
- tokens: bfloat16 [16, 1024, 1152], P('dp', 'tensor'), may hold values from -6 to 6
- conditioning: float32 [16, 1152], P('dp'), may hold values from -12 to 12
- cotangent: bfloat16 [16, 1024, 1152], P('dp', 'tensor'), may hold values from -6 to 6
- query_weight: bfloat16 [1152, 1152], P('dp', 'tensor'), may hold values from -0.20623948 to 0.20623948
- key_weight: bfloat16 [1152, 1152], P('dp', 'tensor'), may hold values from -0.1875 to 0.1875
- value_weight: bfloat16 [1152, 1152], P('dp', 'tensor'), may hold values from -0.1875 to 0.1875
- out_weight: bfloat16 [1152, 1152], P('tensor', 'dp'), may hold values from -1 to 1
- up_weight: bfloat16 [1152, 4608], P('dp', 'tensor'), may hold values from -0.1875 to 0.1875
- down_weight: bfloat16 [4608, 1152], P('tensor', 'dp'), may hold values from -0.09375 to 0.09375
- ada_weight: bfloat16 [1152, 6912], P('dp', 'tensor'), may hold values from -0.109375 to 0.109375
- query_bias: float32 [1152], P('tensor'), may hold values from -3 to 3
- value_bias: float32 [1152], P('tensor'), may hold values from -3 to 3
- out_bias: float32 [1152], replicated, may hold values from -3 to 3
- up_bias: float32 [4608], P('tensor'), may hold values from -3 to 3
- down_bias: float32 [1152], replicated, may hold values from -3 to 3
- ada_bias: float32 [6912], P('tensor'), may hold values from -1.2 to 1.2
- threshold: float32 [1], replicated, may hold values from 0.5 to 1.5
Outputs:
- block_out: bfloat16 [16, 1024, 1152], P('dp', 'tensor')
- grad_tokens: float32 [16, 1024, 1152], P('dp', 'tensor')
- grad_conditioning: float32 [16, 1152], P('dp')
- grad_query_weight: float32 [1152, 1152], P('dp', 'tensor')
- grad_key_weight: float32 [1152, 1152], P('dp', 'tensor')
- grad_value_weight: float32 [1152, 1152], P('dp', 'tensor')
- grad_out_weight: float32 [1152, 1152], P('tensor', 'dp')
- grad_up_weight: float32 [1152, 4608], P('dp', 'tensor')
- grad_down_weight: float32 [4608, 1152], P('tensor', 'dp')
- grad_ada_weight: float32 [1152, 6912], P('dp', 'tensor')
- grad_query_bias: float32 [1152], P('tensor')
- grad_value_bias: float32 [1152], P('tensor')
- grad_out_bias: float32 [1152], replicated
- grad_up_bias: float32 [4608], P('tensor')
- grad_down_bias: float32 [1152], replicated
- grad_ada_bias: float32 [6912], P('tensor')
- query_clipped: bfloat16 [1152, 1152], P('dp', 'tensor')
- key_clipped: bfloat16 [1152, 1152], P('dp', 'tensor')
- query_bias_clipped: float32 [1152], P('tensor')
All inputs are finite; a program needn't handle non-finite values.
Results may differ from a plain program's by a relative error of at most 0.0131.
The roundings to bfloat16 on the way count: a program that leaves them out, or rounds other values in their place, can miss the bound.
Values may be sent and summed in bfloat16 or wider, within the bound.
A program may use at most 192 MiB of HBM per device.

v0:
```python
from functools import partial

import jax
import jax.numpy as jnp
from jax import lax
from jax.sharding import PartitionSpec as P

HEAD_DIM = 72


epsilon = 1e-06


def modulate(values, shift, scale):
    average = jnp.mean(values, axis=-1, keepdims=True)
    centred = values - average
    spread = jnp.mean(centred * centred, axis=-1, keepdims=True)
    return centred * lax.rsqrt(spread + epsilon) * (1.0 + scale[:, None, :]) + shift[:, None, :]


def product(left, right):
    return jnp.dot(left, right, preferred_element_type=jnp.float32)


def inner_rows(left, right):
    return lax.dot_general(
        left, right, (((0,), (0,)), ((), ())), preferred_element_type=jnp.float32
    )


def against(left, right):
    return lax.dot_general(
        left, right, (((1,), (1,)), ((), ())), preferred_element_type=jnp.float32
    )


def spread_rows(values):
    return lax.all_gather(values, "tensor", axis=1, tiled=True)


def fold_rows(values):
    return lax.psum_scatter(values, "tensor", scatter_dimension=1, tiled=True)


def spread_grads(values):
    return lax.all_gather(values, "tensor", axis=1, tiled=True)


def fold_grads(values):
    return lax.psum_scatter(values, "tensor", scatter_dimension=1, tiled=True)


def local(
    tokens,
    conditioning,
    cotangent,
    query_weight,
    key_weight,
    value_weight,
    out_weight,
    up_weight,
    down_weight,
    ada_weight,
    query_bias,
    value_bias,
    out_bias,
    up_bias,
    down_bias,
    ada_bias,
    threshold,
):
    images = tokens.shape[0]
    model_width = tokens.shape[2]
    gathered = (
        lax.all_gather(query_weight, "dp", axis=0, tiled=True),
        lax.all_gather(key_weight, "dp", axis=0, tiled=True),
        lax.all_gather(value_weight, "dp", axis=0, tiled=True),
        lax.all_gather(out_weight, "dp", axis=1, tiled=True),
        lax.all_gather(up_weight, "dp", axis=0, tiled=True),
        lax.all_gather(down_weight, "dp", axis=1, tiled=True),
        lax.all_gather(ada_weight, "dp", axis=0, tiled=True),
    )
    full_query, full_key, full_value, full_out, full_up, full_down, full_ada = gathered
    lifted_low = jax.nn.silu(conditioning).astype(jnp.bfloat16)
    own_columns = product(lifted_low, full_ada) + ada_bias
    modulation = lax.all_gather(own_columns, "tensor", axis=1, tiled=True)
    pieces = [
        modulation[:, piece_index * model_width : (piece_index + 1) * model_width]
        for piece_index in range(6)
    ]
    shift_attn, scale_attn, gate_attn, shift_mlp, scale_mlp, gate_mlp = pieces
    inputs = tokens.astype(jnp.float32)
    normed_attn = spread_rows(modulate(inputs, shift_attn, scale_attn).astype(jnp.bfloat16))
    length = normed_attn.shape[1]
    row_count = images * length
    flat_attn = normed_attn.reshape(row_count, model_width)
    local_width = full_query.shape[1]
    heads_here = local_width // HEAD_DIM
    queries = (product(flat_attn, full_query) + query_bias).astype(jnp.bfloat16)
    key_rows = product(flat_attn, full_key).astype(jnp.bfloat16)
    value_rows = (product(flat_attn, full_value) + value_bias).astype(jnp.bfloat16)
    block_rows = min(512, length)
    head_scale = HEAD_DIM ** (-0.5)

    def by_head(matrix):
        return matrix.reshape(images, length, heads_here, HEAD_DIM)

    def attend_image(bundle):
        queries_img, keys_img, values_img = bundle
        outputs, totals, highest = ([], [], [])
        for offset in range(0, length, block_rows):
            logits = (
                jnp.einsum(
                    "qhe,khe->hqk",
                    queries_img[offset : offset + block_rows],
                    keys_img,
                    preferred_element_type=jnp.float32,
                )
                * head_scale
            )
            row_top = jnp.max(logits, axis=2, keepdims=True)
            raised = jnp.exp(logits - row_top)
            summed = jnp.sum(raised, axis=2, keepdims=True)
            shares = (raised / summed).astype(jnp.bfloat16)
            outputs.append(
                jnp.einsum(
                    "hqk,khe->qhe", shares, values_img, preferred_element_type=jnp.float32
                ).astype(jnp.bfloat16)
            )
            totals.append(row_top[:, :, 0] + jnp.log(summed[:, :, 0]))
            highest.append(jnp.max(row_top[:, :, 0], axis=1))
        return (
            jnp.concatenate(outputs, 0),
            jnp.concatenate(totals, 1),
            jnp.max(jnp.stack(highest), axis=0),
        )

    attended, log_totals, image_peaks = lax.map(
        attend_image, (by_head(queries), by_head(key_rows), by_head(value_rows))
    )
    flat_attended = attended.reshape(row_count, local_width)
    branch_attn = (
        fold_rows(product(flat_attended, full_out).reshape(images, length, model_width)) + out_bias
    )
    after_attn = inputs + gate_attn[:, None, :] * branch_attn
    normed_mlp = spread_rows(modulate(after_attn, shift_mlp, scale_mlp).astype(jnp.bfloat16))
    flat_mlp = normed_mlp.reshape(row_count, model_width)
    upward = product(flat_mlp, full_up) + up_bias
    active = jax.nn.gelu(upward, approximate=True).astype(jnp.bfloat16)
    branch_mlp = (
        fold_rows(product(active, full_down).reshape(images, length, model_width)) + down_bias
    )
    block_out = (after_attn + gate_mlp[:, None, :] * branch_mlp).astype(jnp.bfloat16)
    peaks = lax.pmax(jnp.max(image_peaks, axis=0), "dp")
    again = (
        lax.all_gather(query_weight, "dp", axis=0, tiled=True),
        lax.all_gather(key_weight, "dp", axis=0, tiled=True),
        lax.all_gather(value_weight, "dp", axis=0, tiled=True),
        lax.all_gather(out_weight, "dp", axis=1, tiled=True),
        lax.all_gather(up_weight, "dp", axis=0, tiled=True),
        lax.all_gather(down_weight, "dp", axis=1, tiled=True),
        lax.all_gather(ada_weight, "dp", axis=0, tiled=True),
    )
    back_query, back_key, back_value, back_out, back_up, back_down, back_ada = again
    grad_out = cotangent.astype(jnp.float32)
    grad_branch_mlp = (gate_mlp[:, None, :] * grad_out).astype(jnp.bfloat16)
    grad_gate_mlp = jnp.sum(grad_out * branch_mlp, axis=1)
    flat_grad_mlp = spread_grads(grad_branch_mlp).reshape(row_count, model_width)
    grad_down_bias = jnp.sum(flat_grad_mlp, axis=0, dtype=jnp.float32)
    grad_down_weight = inner_rows(active, flat_grad_mlp)
    grad_active = against(flat_grad_mlp, back_down)
    _, gelu_pull = jax.vjp(partial(jax.nn.gelu, approximate=True), upward)
    grad_upward = gelu_pull(grad_active)[0].astype(jnp.bfloat16)
    grad_up_bias = jnp.sum(grad_upward, axis=0, dtype=jnp.float32)
    grad_up_weight = inner_rows(flat_mlp, grad_upward)
    grad_normed_mlp = fold_grads(against(grad_upward, back_up).reshape(images, length, model_width))
    _, mlp_pull = jax.vjp(modulate, after_attn, shift_mlp, scale_mlp)
    grad_after, grad_shift_mlp, grad_scale_mlp = mlp_pull(grad_normed_mlp)
    grad_after = grad_out + grad_after
    grad_branch_attn = (gate_attn[:, None, :] * grad_after).astype(jnp.bfloat16)
    grad_gate_attn = jnp.sum(grad_after * branch_attn, axis=1)
    flat_grad_attn = spread_grads(grad_branch_attn).reshape(row_count, model_width)
    grad_out_bias = jnp.sum(flat_grad_attn, axis=0, dtype=jnp.float32)
    grad_out_weight = inner_rows(flat_attended, flat_grad_attn)
    grad_attended = against(flat_grad_attn, back_out).astype(jnp.bfloat16)

    def attend_back(bundle):
        queries_img, keys_img, values_img, grads_img, totals_img = bundle
        query_parts = []
        grad_keys_img = jnp.zeros(keys_img.shape, jnp.float32)
        grad_values_img = jnp.zeros(values_img.shape, jnp.float32)
        for offset in range(0, length, block_rows):
            query_block = queries_img[offset : offset + block_rows]
            grad_block = grads_img[offset : offset + block_rows]
            logits = (
                jnp.einsum(
                    "qhe,khe->hqk", query_block, keys_img, preferred_element_type=jnp.float32
                )
                * head_scale
            )
            shares = jnp.exp(logits - totals_img[:, offset : offset + block_rows, None])
            grad_shares = jnp.einsum(
                "qhe,khe->hqk", grad_block, values_img, preferred_element_type=jnp.float32
            )
            row_inner = jnp.sum(shares * grad_shares, axis=2, keepdims=True)
            grad_logits = (shares * (grad_shares - row_inner)).astype(jnp.bfloat16)
            query_parts.append(
                (
                    jnp.einsum(
                        "hqk,khe->qhe", grad_logits, keys_img, preferred_element_type=jnp.float32
                    )
                    * head_scale
                ).astype(jnp.bfloat16)
            )
            grad_keys_img = (
                grad_keys_img
                + jnp.einsum(
                    "hqk,qhe->khe", grad_logits, query_block, preferred_element_type=jnp.float32
                )
                * head_scale
            )
            grad_values_img = grad_values_img + jnp.einsum(
                "hqk,qhe->khe",
                shares.astype(jnp.bfloat16),
                grad_block,
                preferred_element_type=jnp.float32,
            )
        return (
            jnp.concatenate(query_parts, 0),
            grad_keys_img.astype(jnp.bfloat16),
            grad_values_img.astype(jnp.bfloat16),
        )

    grad_queries, grad_keys, grad_values = lax.map(
        attend_back,
        (
            by_head(queries),
            by_head(key_rows),
            by_head(value_rows),
            by_head(grad_attended),
            log_totals,
        ),
    )
    grad_queries = grad_queries.reshape(row_count, local_width)
    grad_keys = grad_keys.reshape(row_count, local_width)
    grad_values = grad_values.reshape(row_count, local_width)
    grad_query_bias = jnp.sum(grad_queries, axis=0, dtype=jnp.float32)
    grad_value_bias = jnp.sum(grad_values, axis=0, dtype=jnp.float32)
    grad_query_weight = inner_rows(flat_attn, grad_queries)
    grad_key_weight = inner_rows(flat_attn, grad_keys)
    grad_value_weight = inner_rows(flat_attn, grad_values)
    partial_normed = (
        against(grad_queries, back_query)
        + against(grad_keys, back_key)
        + against(grad_values, back_value)
    )
    grad_normed_attn = fold_grads(partial_normed.reshape(images, length, model_width))
    _, attn_pull = jax.vjp(modulate, inputs, shift_attn, scale_attn)
    grad_inputs, grad_shift_attn, grad_scale_attn = attn_pull(grad_normed_attn)
    grad_tokens = grad_after + grad_inputs
    modulation_terms = jnp.concatenate(
        [
            grad_shift_attn,
            grad_scale_attn,
            grad_gate_attn,
            grad_shift_mlp,
            grad_scale_mlp,
            grad_gate_mlp,
        ],
        axis=1,
    )
    grad_modulation = lax.psum_scatter(
        modulation_terms, "tensor", scatter_dimension=1, tiled=True
    ).astype(jnp.bfloat16)
    grad_ada_bias = jnp.sum(grad_modulation, axis=0, dtype=jnp.float32)
    grad_ada_weight = inner_rows(lifted_low, grad_modulation)
    grad_lifted = lax.psum(against(grad_modulation, back_ada), "tensor")
    _, silu_pull = jax.vjp(jax.nn.silu, conditioning)
    grad_conditioning = silu_pull(grad_lifted)[0]
    weight_grads = (
        lax.psum_scatter(grad_query_weight, "dp", scatter_dimension=0, tiled=True),
        lax.psum_scatter(grad_key_weight, "dp", scatter_dimension=0, tiled=True),
        lax.psum_scatter(grad_value_weight, "dp", scatter_dimension=0, tiled=True),
        lax.psum_scatter(grad_out_weight, "dp", scatter_dimension=1, tiled=True),
        lax.psum_scatter(grad_up_weight, "dp", scatter_dimension=0, tiled=True),
        lax.psum_scatter(grad_down_weight, "dp", scatter_dimension=1, tiled=True),
        lax.psum_scatter(grad_ada_weight, "dp", scatter_dimension=0, tiled=True),
    )
    bias_grads = lax.psum(
        (
            grad_query_bias,
            grad_value_bias,
            grad_out_bias,
            grad_up_bias,
            grad_down_bias,
            grad_ada_bias,
        ),
        "dp",
    )
    limit = threshold[0]
    factor = jnp.sqrt(limit / jnp.maximum(peaks, limit))
    column_factor = jnp.repeat(factor, HEAD_DIM)
    query_clipped = (query_weight.astype(jnp.float32) * column_factor).astype(jnp.bfloat16)
    key_clipped = (key_weight.astype(jnp.float32) * column_factor).astype(jnp.bfloat16)
    query_bias_clipped = query_bias * column_factor
    return (
        block_out,
        grad_tokens,
        grad_conditioning,
        weight_grads[0],
        weight_grads[1],
        weight_grads[2],
        weight_grads[3],
        weight_grads[4],
        weight_grads[5],
        weight_grads[6],
        bias_grads[0],
        bias_grads[1],
        bias_grads[2],
        bias_grads[3],
        bias_grads[4],
        bias_grads[5],
        query_clipped,
        key_clipped,
        query_bias_clipped,
    )


def solution(mesh):
    in_specs = (
        P("dp", "tensor", None),
        P("dp", None),
        P("dp", "tensor", None),
        P("dp", "tensor"),
        P("dp", "tensor"),
        P("dp", "tensor"),
        P("tensor", "dp"),
        P("dp", "tensor"),
        P("tensor", "dp"),
        P("dp", "tensor"),
        P("tensor"),
        P("tensor"),
        P(),
        P("tensor"),
        P(),
        P("tensor"),
        P(),
    )
    out_specs = (
        P("dp", "tensor", None),
        P("dp", "tensor", None),
        P("dp", None),
        P("dp", "tensor"),
        P("dp", "tensor"),
        P("dp", "tensor"),
        P("tensor", "dp"),
        P("dp", "tensor"),
        P("tensor", "dp"),
        P("dp", "tensor"),
        P("tensor"),
        P("tensor"),
        P(),
        P("tensor"),
        P(),
        P("tensor"),
        P("dp", "tensor"),
        P("dp", "tensor"),
        P("tensor"),
    )
    return jax.shard_map(local, mesh=mesh, in_specs=in_specs, out_specs=out_specs, check_vma=False)
```

profile of v0, /device:TPU:28, one launch (start us, length us, event | category | flops | bytes accessed | tf_op | source)
XLA Modules:
  0.0 1795.0 jit_solution(12185849917782094092)
XLA Ops:
  10.6 36.6 %all-gather.9.cloned.1.call-done = bf16[1152,1728]{1,0:T(8,128)(2,1)} async-done(((bf16[144,1728]{1,0:T(8,128)(2,1)}), bf16[1152,1728]{1,0:T(8,128)(2,1)}) %all-gather.9.cloned.1.call-update) | async-done | bytes 3981328 | tf_op jit(solution)/shard_map/all_gather | solution.py:81
  50.0 13.2 all-gather
  66.3 10.9 all_gather.46
  77.2 11.6 all_gather.49
  88.8 10.5 all_gather.47
  99.3 10.6 all_gather.48
  109.9 43.5 %all-gather.11.cloned.1.call-done = bf16[2,1024,1152]{2,1,0:T(8,128)(2,1)} async-done(((bf16[2,256,1152]{2,1,0:T(8,128)(2,1)}), bf16[2,1024,1152]{2,1,0:T(8,128)(2,1)}) %all-gather.11.cloned.1.call-update) | async-done | bytes 4718608 | tf_op jit(solution)/shard_map/all_gather | solution.py:38
  176.8 37.6 %while.28 = (s32[]{:T(128)}, bf16[2,1024,4,72]{1,3,2,0:T(8,128)(2,1)}, f32[2,4,1024]{2,1,0:T(4,128)}, f32[2,4]{1,0:T(2,128)}, bf16[2,1024,4,72]{1,3,2,0:T(8,128)...) while((s32[]{:T(128)}, ...), condition=%wide.region_9.10_spmd, body=%wide.region_2.9_spmd.sunk | while | flops 1251377152 | bytes 55216892 | solution.py:138
  226.7 158.5 %reduce-scatter.15.cloned.1.call-done = f32[2,256,1152]{2,1,0:T(8,128)} async-done(((f32[2,1024,1152]{2,1,0:T(8,128)}), f32[2,256,1152]{2,1,0:T(8,128)}) %reduce-scatter.15.cloned.1.call-update) | async-done | bytes 2359312 | tf_op jit(solution)/shard_map/reduce_scatter | solution.py:42
  390.7 27.4 %all-gather.17.cloned.1.call-done = bf16[1152,1152]{0,1:T(8,128)(2,1)} async-done(((bf16[1152,144]{0,1:T(8,128)(2,1)}), bf16[1152,1152]{0,1:T(8,128)(2,1)}) %all-gather.17.cloned.1.call-update) | async-done | bytes 2654224 | tf_op jit(solution)/shard_map/all_gather | solution.py:80
  418.1 89.0 %all-gather.19.cloned.1.call-done = bf16[2,1024,1152]{2,1,0:T(8,128)(2,1)} async-done(((bf16[2,256,1152]{2,1,0:T(8,128)(2,1)}), bf16[2,1024,1152]{2,1,0:T(8,128)(2,1)}) %all-gather.19.cloned.1.call-update) | async-done | bytes 4718608 | tf_op jit(solution)/shard_map/all_gather | solution.py:46
  507.1 11.7 fusion.127
  518.8 21.3 %all-gather.15.cloned.1.call-done = bf16[1152,1152]{1,0:T(8,128)(2,1)} async-done(((bf16[144,1152]{1,0:T(8,128)(2,1)}), bf16[1152,1152]{1,0:T(8,128)(2,1)}) %all-gather.15.cloned.1.call-update) | async-done | bytes 2654224 | tf_op jit(solution)/shard_map/all_gather | solution.py:79
  540.0 88.5 %all-gather.13.cloned.1.call-done = bf16[2,1024,1152]{2,1,0:T(8,128)(2,1)} async-done(((bf16[2,256,1152]{2,1,0:T(8,128)(2,1)}), bf16[2,1024,1152]{2,1,0:T(8,128)(2,1)}) %all-gather.13.cloned.1.call-update) | async-done | bytes 4718608 | tf_op jit(solution)/shard_map/all_gather | solution.py:38
  628.6 18.0 %convert_reduce_fusion.1 = (f32[1152]{0:T(1024)}, bf16[2048,1152]{1,0:T(8,128)(2,1)S(1)}, f32[2048,1152]{1,0:T(8,128)}) fusion(f32[2048,1152]{1,0:T(8,128)} %fusion.127, f32[1152]{0:T(1024)S(1)} %copy-done.62, bf16[2048,1152]{1,0:T(8,128)(2,1)} %bitcast.287, bf16[1152,1152]{1,0:T(8,128)(2,1)} %all-gather.15.cloned.1.call-done), kind=kOutput, calls=%fused_computation.118 | convolution fusion | flops 5490080768 | bytes 30974976 | tf_op jit(solution)/shard_map/dot_general | solution.py:22
  655.9 162.2 %reduce-scatter.19.cloned.1.call-done = f32[2,256,1152]{2,1,0:T(8,128)} async-done(((f32[2,1024,1152]{2,1,0:T(8,128)}), f32[2,256,1152]{2,1,0:T(8,128)}) %reduce-scatter.19.cloned.1.call-update) | async-done | bytes 2359312 | tf_op jit(solution)/shard_map/reduce_scatter | solution.py:50
  826.0 87.8 %all-gather.21.cloned.1.call-done = bf16[2,1024,1152]{2,1,0:T(8,128)(2,1)} async-done(((bf16[2,256,1152]{2,1,0:T(8,128)(2,1)}), bf16[2,1024,1152]{2,1,0:T(8,128)(2,1)}) %all-gather.21.cloned.1.call-update) | async-done | bytes 4718608 | tf_op jit(solution)/shard_map/all_gather | solution.py:46
  927.1 65.1 %while.29 = (s32[]{:T(128)}, bf16[2,1024,4,72]{1,3,2,0:T(8,128)(2,1)}, bf16[2,1024,4,72]{1,3,2,0:T(8,128)(2,1)}, bf16[2,1024,4,72]{1,3,2,0:T(8,128)(2,1)}, bf16[...) while((s32[]{:T(128)}, ...), condition=%wide.region_20.21_spmd, body=%wide.region_17.20_spmd.sunk | while | flops 3073470464 | bytes 163143472 | solution.py:234
  1013.0 13.0 fusion.121
  1026.0 147.5 %reduce-scatter.21.cloned.1.call-done = f32[2,256,1152]{2,1,0:T(8,128)} async-done(((f32[2,1024,1152]{2,1,0:T(8,128)}), f32[2,256,1152]{2,1,0:T(8,128)}) %reduce-scatter.21.cloned.1.call-update) | async-done | bytes 2359312 | tf_op jit(solution)/shard_map/reduce_scatter | solution.py:50
  1180.4 157.6 %reduce-scatter.17.cloned.1.call-done = f32[2,256,1152]{2,1,0:T(8,128)} async-done(((f32[2,1024,1152]{2,1,0:T(8,128)}), f32[2,256,1152]{2,1,0:T(8,128)}) %reduce-scatter.17.cloned.1.call-update) | async-done | bytes 2359312 | tf_op jit(solution)/shard_map/reduce_scatter | solution.py:42
  1350.0 12.5 fusion.134
  1363.0 14.0 fusion.120
  1405.7 11.1 reduce-scatter.37.cloned.1.call-done
  1424.1 12.7 pmax.7
  1446.8 24.1 %all-reduce = (f32[288]{0:T(512)}, f32[288]{0:T(512)}, f32[1152]{0:T(1024)}, f32[1152]{0:T(1024)}, f32[1152]{0:T(1024)}, /*index=5*/f32[1728]{0:T(1024)}) all-reduce(f32[288]{0:T(512)S(1)} %reduce_sum.248, f32[288]{0:T(512)S(1)} %reduce_sum.250, f32[1152]{0:T(1024)S(1)} %convert_reduce_fusion.2, ...), channel_id=1, replica_groups=mesh['dp'=8,'tensor'=4] {'dp'}, use_global_device_ids=true, to_apply=%region_40.41 | all-reduce | flops 5760 | bytes 46080 | tf_op jit(solution)/shard_map/psum | solution.py:289
  1483.9 56.7 %reduce-scatter.33.cloned.1.call-done = f32[1152,144]{0,1:T(8,128)} async-done(((f32[1152,1152]{0,1:T(8,128)}), f32[1152,144]{0,1:T(8,128)}) %reduce-scatter.33.cloned.1.call-update) | async-done | bytes 663568 | tf_op jit(solution)/shard_map/reduce_scatter | solution.py:286
  1540.5 43.3 %reduce-scatter.29.cloned.1.call-done = f32[288,144]{0,1:T(8,128)} async-done(((f32[288,1152]{0,1:T(8,128)}), f32[288,144]{0,1:T(8,128)}) %reduce-scatter.29.cloned.1.call-update) | async-done | bytes 165904 | tf_op jit(solution)/shard_map/reduce_scatter | solution.py:284
  1583.8 43.2 %reduce-scatter.27.cloned.1.call-done = f32[144,288]{1,0:T(8,128)} async-done(((f32[1152,288]{1,0:T(8,128)}), f32[144,288]{1,0:T(8,128)}) %reduce-scatter.27.cloned.1.call-update) | async-done | bytes 165904 | tf_op jit(solution)/shard_map/reduce_scatter | solution.py:283
  1627.0 43.2 %reduce-scatter.25.cloned.1.call-done = f32[144,288]{1,0:T(8,128)} async-done(((f32[1152,288]{1,0:T(8,128)}), f32[144,288]{1,0:T(8,128)}) %reduce-scatter.25.cloned.1.call-update) | async-done | bytes 165904 | tf_op jit(solution)/shard_map/reduce_scatter | solution.py:282
  1670.2 43.2 %reduce-scatter.23.cloned.1.call-done = f32[144,288]{1,0:T(8,128)} async-done(((f32[1152,288]{1,0:T(8,128)}), f32[144,288]{1,0:T(8,128)}) %reduce-scatter.23.cloned.1.call-update) | async-done | bytes 165904 | tf_op jit(solution)/shard_map/reduce_scatter | solution.py:281
  1713.5 74.9 %reduce-scatter.35.cloned.1.call-done = f32[144,1728]{1,0:T(8,128)} async-done(((f32[1152,1728]{1,0:T(8,128)}), f32[144,1728]{1,0:T(8,128)}) %reduce-scatter.35.cloned.1.call-update) | async-done | bytes 995344 | tf_op jit(solution)/shard_map/reduce_scatter | solution.py:287
  (313 shorter events, 280.4 us)
Async XLA Ops:
  7.2 40.0 %copy-start.40 = (f32[2,1152]{1,0:T(2,128)S(1)}, f32[2,1152]{1,0:T(2,128)}, u32[]{:S(2)}) copy-start(f32[2,1152]{1,0:T(2,128)} %param.22) | copy-start | bytes 27652
  7.2 40.0 %copy-start.55 = (f32[1728]{0:T(1024)S(1)}, f32[1728]{0:T(1024)}, u32[]{:S(2)}) copy-start(f32[1728]{0:T(1024)} %param.36) | copy-start | bytes 20740
  7.2 40.0 %all-gather.9.cloned.1.call-start = ((), (), s32[]{:S(2)}) async-start(), calls=%async_computation.12 | async-start | bytes 4644864 | tf_op jit(solution)/shard_map/all_gather | solution.py:81
  8.0 145.4 %all-gather.11.cloned.1.call-start = ((), (), s32[]{:S(2)}) async-start(), calls=%async_computation.13 | async-start | bytes 5898240 | tf_op jit(solution)/shard_map/all_gather | solution.py:38
  9.5 54.5 %copy-start.46 = (f32[2,256]{1,0:T(2,128)}, f32[2,256]{1,0:T(2,128)S(1)}, u32[]{:S(2)}) copy-start(f32[2,256]{1,0:T(2,128)S(1)} %broadcast_multiply_fusion.1) | copy-start | bytes 6148
  10.6 55.6 %copy-start.51 = (f32[2,256]{1,0:T(2,128)}, f32[2,256]{1,0:T(2,128)S(1)}, u32[]{:S(2)}) copy-start(f32[2,256]{1,0:T(2,128)S(1)} %fusion.114) | copy-start | bytes 6148
  66.2 319.0 %reduce-scatter.15.cloned.1.call-start = ((), (), s32[]{:S(2)}) async-start(), calls=%async_computation.14 | async-start | bytes 11796480 | tf_op jit(solution)/shard_map/reduce_scatter | solution.py:42
  99.3 62.8 %copy-start.26 = (bf16[1152,288]{1,0:T(8,128)(2,1)}, bf16[1152,288]{1,0:T(8,128)(2,1)S(1)}, u32[]{:S(2)}) copy-start(bf16[1152,288]{1,0:T(8,128)(2,1)S(1)} %all_gather.47) | copy-start | bytes 1990660
  109.9 48.6 %copy-start.31 = (bf16[1152,288]{1,0:T(8,128)(2,1)}, bf16[1152,288]{1,0:T(8,128)(2,1)S(1)}, u32[]{:S(2)}) copy-start(bf16[1152,288]{1,0:T(8,128)(2,1)S(1)} %all_gather.48) | copy-start | bytes 1990660
  222.9 162.3 %copy-start.4 = (bf16[2,256,1152]{2,1,0:T(8,128)(2,1)S(1)}, bf16[2,256,1152]{2,1,0:T(8,128)(2,1)}, u32[]{:S(2)}) copy-start(bf16[2,256,1152]{2,1,0:T(8,128)(2,1)} %param.21) | copy-start | bytes 3538948
  222.9 195.2 %all-gather.17.cloned.1.call-start = ((), (), s32[]{:S(2)}) async-start(), calls=%async_computation.17 | async-start | bytes 2985984 | tf_op jit(solution)/shard_map/all_gather | solution.py:80
  223.5 283.6 %all-gather.19.cloned.1.call-start = ((), (), s32[]{:S(2)}) async-start(), calls=%async_computation.19 | async-start | bytes 5898240 | tf_op jit(solution)/shard_map/all_gather | solution.py:46
  226.1 314.0 %all-gather.15.cloned.1.call-start = ((), (), s32[]{:S(2)}) async-start(), calls=%async_computation.16 | async-start | bytes 2985984 | tf_op jit(solution)/shard_map/all_gather | solution.py:79
  226.7 401.9 %all-gather.13.cloned.1.call-start = ((), (), s32[]{:S(2)}) async-start(), calls=%async_computation.15 | async-start | bytes 5898240 | tf_op jit(solution)/shard_map/all_gather | solution.py:38
  390.2 427.9 %reduce-scatter.19.cloned.1.call-start = ((), (), s32[]{:S(2)}) async-start(), calls=%async_computation.20 | async-start | bytes 11796480 | tf_op jit(solution)/shard_map/reduce_scatter | solution.py:50
  507.1 121.5 %copy-start.62 = (f32[1152]{0:T(1024)S(1)}, f32[1152]{0:T(1024)}, u32[]{:S(2)}) copy-start(f32[1152]{0:T(1024)} %param.34) | copy-start | bytes 13828
  655.9 258.0 %all-gather.21.cloned.1.call-start = ((), (), s32[]{:S(2)}) async-start(), calls=%async_computation.21 | async-start | bytes 5898240 | tf_op jit(solution)/shard_map/all_gather | solution.py:46
  824.4 89.5 %copy-start.28 = (bf16[288,1152]{0,1:T(8,128)(2,1)S(1)}, bf16[288,1152]{0,1:T(8,128)(2,1)}, u32[]{:S(2)}) copy-start(bf16[288,1152]{0,1:T(8,128)(2,1)} %all_gather.49) | copy-start | bytes 1990660
  825.8 347.7 %reduce-scatter.21.cloned.1.call-start = ((), (), s32[]{:S(2)}) async-start(), calls=%async_computation.22 | async-start | bytes 11796480 | tf_op jit(solution)/shard_map/reduce_scatter | solution.py:50
  1011.2 326.8 %reduce-scatter.17.cloned.1.call-start = ((), (), s32[]{:S(2)}) async-start(), calls=%async_computation.18 | async-start | bytes 11796480 | tf_op jit(solution)/shard_map/reduce_scatter | solution.py:42
  1025.9 147.6 %copy-start.5 = (bf16[2,256,1152]{2,1,0:T(8,128)(2,1)S(1)}, bf16[2,256,1152]{2,1,0:T(8,128)(2,1)}, u32[]{:S(2)}) copy-start(bf16[2,256,1152]{2,1,0:T(8,128)(2,1)} %param.21) | copy-start | bytes 3538948
  1025.9 147.6 %copy-start.38 = (f32[2,1152]{1,0:T(2,128)S(1)}, f32[2,1152]{1,0:T(2,128)}, u32[]{:S(2)}) copy-start(f32[2,1152]{1,0:T(2,128)} %copy-done.37) | copy-start | bytes 27652
  1025.9 147.6 %copy-start.47 = (f32[2,256]{1,0:T(2,128)S(1)}, f32[2,256]{1,0:T(2,128)}, u32[]{:S(2)}) copy-start(f32[2,256]{1,0:T(2,128)} %copy-done.46) | copy-start | bytes 6148
  1026.0 390.8 %reduce-scatter.37.cloned.1.call-start = ((), (), s32[]{:S(2)}) async-start(), calls=%async_computation.30 | async-start | bytes 4423680
  1175.9 162.2 %copy-start.2 = (f32[2,256,1152]{2,1,0:T(8,128)S(1)}, f32[2,256,1152]{2,1,0:T(8,128)}, u32[]{:S(2)}) copy-start(f32[2,256,1152]{2,1,0:T(8,128)} %copy-done) | copy-start | bytes 7077892
  1349.9 133.9 %reduce-scatter.31.cloned.1.call-start = ((), (), s32[]{:S(2)}) async-start(), calls=%async_computation.27 | async-start | bytes 5971968 | tf_op jit(solution)/shard_map/reduce_scatter | solution.py:285
  1362.5 178.0 %reduce-scatter.33.cloned.1.call-start = ((), (), s32[]{:S(2)}) async-start(), calls=%async_computation.28 | async-start | bytes 5971968 | tf_op jit(solution)/shard_map/reduce_scatter | solution.py:286
  1377.0 206.8 %reduce-scatter.29.cloned.1.call-start = ((), (), s32[]{:S(2)}) async-start(), calls=%async_computation.26 | async-start | bytes 1990656 | tf_op jit(solution)/shard_map/reduce_scatter | solution.py:284
  1386.2 240.8 %reduce-scatter.27.cloned.1.call-start = ((), (), s32[]{:S(2)}) async-start(), calls=%async_computation.25 | async-start | bytes 1990656 | tf_op jit(solution)/shard_map/reduce_scatter | solution.py:283
  1392.9 277.4 %reduce-scatter.25.cloned.1.call-start = ((), (), s32[]{:S(2)}) async-start(), calls=%async_computation.24 | async-start | bytes 1990656 | tf_op jit(solution)/shard_map/reduce_scatter | solution.py:282
  1399.3 314.2 %reduce-scatter.23.cloned.1.call-start = ((), (), s32[]{:S(2)}) async-start(), calls=%async_computation.23 | async-start | bytes 1990656 | tf_op jit(solution)/shard_map/reduce_scatter | solution.py:281
  1405.6 382.7 %reduce-scatter.35.cloned.1.call-start = ((), (), s32[]{:S(2)}) async-start(), calls=%async_computation.29 | async-start | bytes 9289728 | tf_op jit(solution)/shard_map/reduce_scatter | solution.py:287
  (57 other events, 304.6 us)
Sparse Core Ops, SparseCore 0:
  9.9 37.2 all-gather.8
  66.3 86.9 all-gather.10
  223.0 162.1 reduce-scatter.14
  386.9 31.1 all-gather.16
  420.1 86.9 all-gather.18
  508.8 31.1 all-gather.14
  541.6 86.9 all-gather.12
  656.0 162.1 reduce-scatter.18
  825.9 87.8 all-gather.20
  1011.4 162.1 reduce-scatter.20
  1175.9 162.1 reduce-scatter.16
  1350.1 66.6 reduce-scatter.36
  1420.8 58.5 reduce-scatter.30
  1483.6 56.8 reduce-scatter.32
  1544.3 39.4 reduce-scatter.28
  1587.6 39.4 reduce-scatter.26
  1630.8 39.3 reduce-scatter.24
  1674.0 39.3 reduce-scatter.22
  1717.7 70.5 reduce-scatter.34
where the time goes:
time: 1800 us
  waiting for transfers between devices  1340 us (74%)
  matrix products  211 us (12%)
  blocking collectives  103 us (6%)
  other arithmetic  72.6 us (4%)
  local copies, waits for them, and re-layouts  52.8 us (3%)
    reduce_scatter x2, waiting for transfers between devices, fold_rows(): return lax.psum_scatter(values, 'tensor', scatter_dimension=1, tiled=True)  316 us
    reduce_scatter x2, waiting for transfers between devices, fold_grads(): return lax.psum_scatter(values, 'tensor', scatter_dimension=1, tiled=True)  310 us
    all_gather x2, waiting for transfers between devices, spread_grads(): return lax.all_gather(values, 'tensor', axis=1, tiled=True)  177 us
    all_gather x2, waiting for transfers between devices, spread_rows(): return lax.all_gather(values, 'tensor', axis=1, tiled=True)  132 us
    reduce_scatter x1, waiting for transfers between devices, local(): lax.psum_scatter(grad_ada_weight, 'dp', scatter_dimension=0, tiled=True)  74.9 us
    reduce_scatter x1, waiting for transfers between devices, local(): lax.psum_scatter(grad_down_weight, 'dp', scatter_dimension=1, tiled=True)  56.7 us
    dot_general x7, matrix products, inner_rows(): lax.dot_general(left, right, (((0,), (0,)), ((), ())), preferred_element_...  56.4 us
    dot_general x7, matrix products, product(): return jnp.dot(left, right, preferred_element_type=jnp.float32)  55.5 us
  transfers between devices with their start and end apart: 19, of which 18 were waited for; matrix products, arithmetic and copies ran while one was open for 6% of the time, Pallas kernels for 0%

commit v1 on v0

--- a/solution.py
+++ b/solution.py
@@ -1,17 +1,18 @@
+import functools
 from functools import partial
 
 import jax
 import jax.numpy as jnp
 from jax import lax
-from jax.sharding import PartitionSpec as P
+from jax.experimental import pallas as pl
+from jax.experimental.pallas import tpu as pltpu
+from jax.sharding import Mesh, PartitionSpec as P
 
 HEAD_DIM = 72
-
-
 epsilon = 1e-06
-
-
-def modulate(values, shift, scale):
+partial_gelu = partial(jax.nn.gelu, approximate=True)
+
+def modulate_images(values, shift, scale):
     average = jnp.mean(values, axis=-1, keepdims=True)
     centred = values - average
     spread = jnp.mean(centred * centred, axis=-1, keepdims=True)
@@ -90,7 +91,7 @@
     ]
     shift_attn, scale_attn, gate_attn, shift_mlp, scale_mlp, gate_mlp = pieces
     inputs = tokens.astype(jnp.float32)
-    normed_attn = spread_rows(modulate(inputs, shift_attn, scale_attn).astype(jnp.bfloat16))
+    normed_attn = spread_rows(modulate_images(inputs, shift_attn, scale_attn).astype(jnp.bfloat16))
     length = normed_attn.shape[1]
     row_count = images * length
     flat_attn = normed_attn.reshape(row_count, model_width)
@@ -143,7 +144,7 @@
         fold_rows(product(flat_attended, full_out).reshape(images, length, model_width)) + out_bias
     )
     after_attn = inputs + gate_attn[:, None, :] * branch_attn
-    normed_mlp = spread_rows(modulate(after_attn, shift_mlp, scale_mlp).astype(jnp.bfloat16))
+    normed_mlp = spread_rows(modulate_images(after_attn, shift_mlp, scale_mlp).astype(jnp.bfloat16))
     flat_mlp = normed_mlp.reshape(row_count, model_width)
     upward = product(flat_mlp, full_up) + up_bias
     active = jax.nn.gelu(upward, approximate=True).astype(jnp.bfloat16)
@@ -174,7 +175,7 @@
     grad_up_bias = jnp.sum(grad_upward, axis=0, dtype=jnp.float32)
     grad_up_weight = inner_rows(flat_mlp, grad_upward)
     grad_normed_mlp = fold_grads(against(grad_upward, back_up).reshape(images, length, model_width))
-    _, mlp_pull = jax.vjp(modulate, after_attn, shift_mlp, scale_mlp)
+    _, mlp_pull = jax.vjp(modulate_images, after_attn, shift_mlp, scale_mlp)
     grad_after, grad_shift_mlp, grad_scale_mlp = mlp_pull(grad_normed_mlp)
     grad_after = grad_out + grad_after
     grad_branch_attn = (gate_attn[:, None, :] * grad_after).astype(jnp.bfloat16)
@@ -255,7 +256,7 @@
         + against(grad_values, back_value)
     )
     grad_normed_attn = fold_grads(partial_normed.reshape(images, length, model_width))
-    _, attn_pull = jax.vjp(modulate, inputs, shift_attn, scale_attn)
+    _, attn_pull = jax.vjp(modulate_images, inputs, shift_attn, scale_attn)
     grad_inputs, grad_shift_attn, grad_scale_attn = attn_pull(grad_normed_attn)
     grad_tokens = grad_after + grad_inputs
     modulation_terms = jnp.concatenate(
@@ -326,45 +327,596 @@
     )
 
 
+MESH = pl.DeviceIdType.MESH
+AXES=("y","x","core","z")
+
+class Net:
+    def __init__(self):
+        self.y,self.x,self.c,self.z=(lax.axis_index(a) for a in AXES)
+        y,x,c,z=self.y,self.x,self.c,self.z
+        self.zp=lax.rem(z+1,4); self.zm=lax.rem(z+3,4); self.zo=lax.rem(z+2,4)
+        self.xn=(y,1-x,c,z); self.yn=(1-y,x,c,z); self.cn=(y,x,1-c,z)
+        self.zpn=(y,x,c,self.zp); self.zmn=(y,x,c,self.zm)
+
+def enter(net, column):
+    bar=pltpu.get_barrier_semaphore()
+    y,x,c,z=net.y,net.x,net.c,net.z
+    others=[net.xn,net.yn]
+    if column:
+        for dc in range(2):
+            for dz in range(4):
+                if dc or dz: others.append((y,x,lax.rem(c+dc,2),lax.rem(z+dz,4)))
+    else:
+        others+= [net.cn,net.zpn,net.zmn]
+    for o in others: pl.semaphore_signal(bar,inc=1,device_id=o,device_id_type=MESH)
+    pl.semaphore_wait(bar,len(others))
+
+ROWS=144; COLS=1152; TOP=80
+
+def gather_kernel(tensors, s_ref, tok_ref, cot_ref, g0, g1, g2, tok_out, cot_out, send, recv, tsend, trecv, lsem):
+    g_refs=(g0,g1,g2)
+    net=Net(); y,x,c,z=net.y,net.x,net.c,net.z
+    enter(net, True)
+    def token_copies(start):
+        for a,(src,dst) in enumerate(((tok_ref,tok_out),(cot_ref,cot_out))):
+            for i in range(2):
+                dc=lax.div(z,2); dz=2*c+i
+                here=jnp.logical_and(dc==c,dz==z)
+                rows=pl.ds(pl.multiple_of(lax.rem(z,2)*256,256),256)
+                cp=pltpu.make_async_remote_copy(src_ref=src.at[i],dst_ref=dst.at[rows],send_sem=tsend.at[a,i],recv_sem=trecv.at[a,lax.rem(z,2)],device_id=(y,x,dc,dz),device_id_type=MESH)
+                lc=pltpu.make_async_copy(src.at[i],dst.at[rows],trecv.at[a,lax.rem(z,2)])
+                @pl.when(jnp.logical_not(here))
+                def _():
+                    if start: cp.start()
+                    else: cp.wait_send()
+                @pl.when(here)
+                def _():
+                    if start: lc.start()
+    def token_arrivals():
+        for a,(src,dst) in enumerate(((tok_ref,tok_out),(cot_ref,cot_out))):
+            for k in range(2):
+                rows=pl.ds(k*256,256)
+                pltpu.make_async_copy(src.at[0],dst.at[rows],trecv.at[a,k]).wait()
+    def slot(t,yy,xx,cc,zz,part=None):
+        row=(4*yy+2*xx+cc)*ROWS
+        n=ROWS
+        if part==0: n=TOP
+        if part==1: row=row+TOP; n=ROWS-TOP
+        return g_refs[t].at[pl.ds(pl.multiple_of(row,16),n),pl.ds(pl.multiple_of(zz*COLS,COLS),COLS)]
+    counter=[0]
+    started=[]
+    def sem_of(t,yy,xx,cc,zz,part):
+        return recv.at[t,4*yy+2*xx+cc,zz,part or 0]
+    def put(dev,t,yy,xx,cc,zz,part=None,own=False):
+        src=s_ref.at[t] if own else slot(t,yy,xx,cc,zz,part)
+        cp=pltpu.make_async_remote_copy(src_ref=src,dst_ref=slot(t,yy,xx,cc,zz,part),send_sem=send.at[counter[0]],recv_sem=sem_of(t,yy,xx,cc,zz,part),device_id=dev,device_id_type=MESH)
+        counter[0]+=1
+        cp.start(); started.append(cp)
+    def arrived(t,yy,xx,cc,zz,part=None):
+        s=slot(t,yy,xx,cc,zz,part)
+        pltpu.make_async_copy(s,s,sem_of(t,yy,xx,cc,zz,part)).wait()
+    def finish():
+        for cp in started: cp.wait_send()
+        started.clear(); counter[0]=0
+    def from_partner(cc):
+        for t in range(tensors):
+            for k in range(4):
+                zz=lax.rem(z+k,4)
+                for yy in range(2):
+                    for xx in range(2):
+                        arrived(t,yy,xx,cc,zz)
+    local=[pltpu.make_async_copy(s_ref.at[t],slot(t,y,x,c,z),lsem.at[t]) for t in range(tensors)]
+    for cp in local: cp.start()
+    token_copies(True)
+    first=(y,1-x); second=(1-y,x)
+    def flow(cc):
+        near=net.xn if cc==0 else net.yn
+        far=net.yn if cc==0 else net.xn
+        nearp=(y,1-x) if cc==0 else (1-y,x)
+        farp=(1-y,x) if cc==0 else (y,1-x)
+        def when(cond,fn):
+            pl.when(cond)(fn)
+        up=z<3; down=z>0
+        def zput(dev,cond,t,zz,own=False):
+            src=s_ref.at[t] if own else slot(t,y,x,cc,zz)
+            cp=pltpu.make_async_remote_copy(src_ref=src,dst_ref=slot(t,y,x,cc,zz),send_sem=send.at[counter[0]],recv_sem=sem_of(t,y,x,cc,zz,None),device_id=dev,device_id_type=MESH)
+            counter[0]+=1
+            pl.when(cond)(cp.start); guarded.append((cond,cp))
+        guarded=[]
+        zpn=(y,x,cc,lax.rem(z+1,4)); zmn=(y,x,cc,lax.rem(z+3,4))
+        for t in range(tensors):
+            put(near,t,y,x,cc,z,own=True); put(far,t,y,x,cc,z,own=True)
+            zput(zpn,up,t,z,own=True); zput(zmn,down,t,z,own=True)
+            put(net.cn,t,y,x,cc,z,own=True)
+        def spread(t,zz):
+            put(near,t,y,x,cc,zz); put(far,t,y,x,cc,zz); put(net.cn,t,y,x,cc,zz)
+        def onward(t,zz):
+            arrived(t,nearp[0],nearp[1],cc,zz); put(far,t,nearp[0],nearp[1],cc,zz); put(net.cn,t,nearp[0],nearp[1],cc,zz)
+            arrived(t,farp[0],farp[1],cc,zz); put(net.cn,t,farp[0],farp[1],cc,zz)
+        def nth(k):
+            if k==0: return z
+            table=((1,2,3),(0,2,3),(3,1,0),(2,1,0))
+            return sum(jnp.where(z==i,table[i][k-1],0) for i in range(4))
+        for k in range(1,4):
+            zz=nth(k)
+            for t in range(tensors):
+                arrived(t,y,x,cc,zz)
+                zput(zpn,jnp.logical_and(zz<z,up),t,zz)
+                zput(zmn,jnp.logical_and(zz>z,down),t,zz)
+                spread(t,zz)
+            for t in range(tensors): onward(t,nth(k-1))
+        for t in range(tensors): onward(t,nth(3))
+        for k in range(4):
+            for t in range(tensors):
+                arrived(t,1-y,1-x,cc,nth(k)); put(net.cn,t,1-y,1-x,cc,nth(k))
+        from_partner(1-cc)
+        for cond,cp in guarded: pl.when(cond)(cp.wait_send)
+        finish()
+    @pl.when(c==0)
+    def _(): flow(0)
+    @pl.when(c==1)
+    def _(): flow(1)
+    for cp in local: cp.wait()
+    token_arrivals()
+    token_copies(False)
+
+def gather(s,tok,cot):
+    T=s.shape[0]
+    hbm=pl.BlockSpec(memory_space=pl.ANY)
+    return pl.pallas_call(functools.partial(gather_kernel,T),
+      out_shape=(jax.ShapeDtypeStruct((8*ROWS,4*COLS),jnp.bfloat16),)*3+(jax.ShapeDtypeStruct((512,COLS),tok.dtype),jax.ShapeDtypeStruct((512,COLS),cot.dtype)),
+      in_specs=[hbm]*3,out_specs=(hbm,)*5,
+      scratch_shapes=[pltpu.SemaphoreType.DMA((40*T,)),pltpu.SemaphoreType.DMA((T,8,4,2)),pltpu.SemaphoreType.DMA((2,2)),pltpu.SemaphoreType.DMA((2,2)),pltpu.SemaphoreType.DMA((T,))],
+      compiler_params=pltpu.CompilerParams(collective_id=1,has_side_effects=True))(s,tok,cot)
+HEAD_DIM=72; HS=288; KV0=256; KVW=640; AT0=768; ATW=384
+C=HEAD_DIM**-0.5; LOG2E=1.4426950408889634
+TOK=512
+bf=jnp.bfloat16; f32=jnp.float32
+
+def dg(a,b,ca,cb): return lax.dot_general(a,b,(((ca,),(cb,)),((),())),preferred_element_type=f32)
+
+def partner():
+    y,x,c,z=(lax.axis_index(a) for a in ("y","x","core","z"))
+    return (y,x,1-c,z)
+
+def greet_partner(dev):
+    bar=pltpu.get_barrier_semaphore()
+    pl.semaphore_signal(bar,inc=1,device_id=dev,device_id_type=MESH)
+    pl.semaphore_wait(bar,1)
+
+def att_fwd_kernel(x_ref,g0_ref,bias_ref,qkv_ref,kvo_ref,att_ref,lse_ref,peak_ref,branch_ref,w,qh,kh,vh,oh,wsem,ssem,rsem):
+    dev=partner()
+    for z in range(4): pltpu.make_async_copy(g0_ref.at[:,pl.ds(z*COLS,COLS)],w.at[z],wsem.at[z]).start()
+    greet_partner(dev)
+    def send(z):
+        return pltpu.make_async_remote_copy(src_ref=qkv_ref.at[z,:,pl.ds(KV0,KVW)],dst_ref=kvo_ref.at[z],send_sem=ssem.at[z],recv_sem=rsem.at[z],device_id=dev,device_id_type=MESH)
+    for z in range(4):
+        pltpu.make_async_copy(g0_ref.at[:,pl.ds(z*COLS,COLS)],w.at[z],wsem.at[z]).wait()
+        def tile(i,_):
+            cols=pl.ds(pl.multiple_of(i*384,384),384)
+            qkv_ref[z,:,cols]=(dg(x_ref[...],w[z,:,cols],1,0)+bias_ref[z,:,cols]).astype(bf)
+            return 0
+        lax.fori_loop(0,3,tile,0)
+        send(z).start()
+    branch_ref[...]=jnp.zeros_like(branch_ref)
+    def chunk(z,_):
+        send(z).wait_recv()
+        for j in range(4):
+            a=j*HEAD_DIM
+            qh[j]=qkv_ref[z,:,a:a+HEAD_DIM]
+            kh[j,:TOK]=qkv_ref[z,:,HS+a:HS+a+HEAD_DIM]
+            vh[j,:TOK]=qkv_ref[z,:,2*HS+a:2*HS+a+HEAD_DIM]
+            kh[j,TOK:]=kvo_ref[z,:,HS-KV0+a:HS-KV0+a+HEAD_DIM]
+            vh[j,TOK:]=kvo_ref[z,:,2*HS-KV0+a:2*HS-KV0+a+HEAD_DIM]
+        def head(j,_):
+            h=z*4+j
+            s=dg(kh[j],qh[j],1,1)
+            m=jnp.max(s,axis=0,keepdims=True)
+            p=jnp.exp2((s-m)*(C*LOG2E))
+            l=jnp.sum(p,axis=0,keepdims=True)
+            o=dg(vh[j],p.astype(bf),0,0)/l
+            oh[j]=o.T.astype(bf)
+            lse_ref[h]=m*(C*LOG2E)+jnp.log2(l)
+            peak_ref[h]=jnp.broadcast_to(jnp.max(m,axis=1,keepdims=True)*C,(1,128))
+            return 0
+        lax.fori_loop(0,4,head,0)
+        att_ref[z]=jnp.concatenate([jnp.zeros((TOK,ATW-HS),bf)]+[oh[j] for j in range(4)],axis=1)
+        def tile(i,_):
+            cols=pl.ds(pl.multiple_of(i*384,384),384)
+            branch_ref[:,cols]+=dg(att_ref[z],w[z,cols,AT0:],1,1)
+            return 0
+        lax.fori_loop(0,3,tile,0)
+        return 0
+    lax.fori_loop(0,4,chunk,0)
+    for z in range(4): send(z).wait_send()
+
+VM=pl.BlockSpec(memory_space=pltpu.VMEM); HB=pl.BlockSpec(memory_space=pl.ANY)
+S=jax.ShapeDtypeStruct
+def att_fwd(x,g0,bias):
+    D=pltpu.SemaphoreType.DMA
+    return pl.pallas_call(att_fwd_kernel,name="att_fwd",
+      out_shape=(S((4,TOK,COLS),bf),S((4,TOK,KVW),bf),S((4,TOK,ATW),bf),S((16,1,TOK),f32),S((16,1,128),f32),S((TOK,COLS),f32)),
+      in_specs=[VM,HB,VM],out_specs=(VM,)*6,
+      scratch_shapes=[pltpu.VMEM((4,COLS,COLS),bf),pltpu.VMEM((4,TOK,HEAD_DIM),bf),pltpu.VMEM((4,2*TOK,HEAD_DIM),bf),pltpu.VMEM((4,2*TOK,HEAD_DIM),bf),pltpu.VMEM((4,TOK,HEAD_DIM),bf),D((4,)),D((4,)),D((4,))],
+      compiler_params=pltpu.CompilerParams(collective_id=3,has_side_effects=True,vmem_limit_bytes=58*2**20))(x,g0,bias)
+
+def att_bwd_kernel(x_ref,gb_ref,g0_ref,qkv_ref,kvo_ref,att_ref,lse_ref,d0_ref,gx_ref,bsum_ref,w,qh,kh,vh,gh,dqh,dkh,dvh,mate_out,mate_in,pack,xt,gt,dbuf,wsem,ssem,rsem,dsem):
+    dev=partner()
+    def load(z): return pltpu.make_async_copy(g0_ref.at[:,pl.ds(pl.multiple_of(z*COLS,COLS),COLS)],w.at[lax.rem(z,2)],wsem.at[lax.rem(z,2)])
+    load(0).start()
+    greet_partner(dev)
+    xt[...]=x_ref[...].T
+    gt[...]=gb_ref[...].T
+    gx_ref[...]=jnp.zeros_like(gx_ref)
+    def send(z):
+        return pltpu.make_async_remote_copy(src_ref=mate_out.at[z],dst_ref=mate_in.at[z],send_sem=ssem.at[z],recv_sem=rsem.at[z],device_id=dev,device_id_type=MESH)
+    def store(z):
+        return pltpu.make_async_copy(dbuf.at[lax.rem(z,2)],d0_ref.at[:,pl.ds(pl.multiple_of(z*COLS,COLS),COLS)],dsem.at[lax.rem(z,2)])
+    def chunk(z,_):
+        k2=lax.rem(z,2)
+        load(z).wait()
+        pl.when(z<3)(lambda: load(z+1).start())
+        ga=dg(gb_ref[...],w[k2,:,AT0:],1,0).astype(bf)
+        for j in range(4):
+            a=j*HEAD_DIM
+            gh[j]=ga[:,ATW-HS+a:ATW-HS+a+HEAD_DIM]
+            qh[j]=qkv_ref[z,:,a:a+HEAD_DIM]
+            kh[j,:TOK]=qkv_ref[z,:,HS+a:HS+a+HEAD_DIM]
+            vh[j,:TOK]=qkv_ref[z,:,2*HS+a:2*HS+a+HEAD_DIM]
+            kh[j,TOK:]=kvo_ref[z,:,HS-KV0+a:HS-KV0+a+HEAD_DIM]
+            vh[j,TOK:]=kvo_ref[z,:,2*HS-KV0+a:2*HS-KV0+a+HEAD_DIM]
+        def head(j,_):
+            k=kh[j]; q=qh[j]; g=gh[j]
+            p=jnp.exp2(dg(k,q,1,1)*(C*LOG2E)-lse_ref[z*4+j])
+            t=p*dg(vh[j],g,1,1)
+            inner=jnp.sum(t,axis=0,keepdims=True)
+            ds=(t-p*inner).astype(bf)
+            dvh[j]=dg(p.astype(bf),g,1,0)
+            dkh[j]=dg(ds,q,1,0)*C
+            dqh[j]=(dg(k,ds,0,0)*C).T.astype(bf)
+            return 0
+        lax.fori_loop(0,4,head,0)
+        mate_out[z]=jnp.concatenate([dkh[j,TOK:].astype(bf) for j in range(4)]+[dvh[j,TOK:].astype(bf) for j in range(4)]+[jnp.zeros((TOK,KVW-2*HS),bf)],axis=1)
+        send(z).start()
+        send(z).wait_recv()
+        o=mate_in[z].astype(f32)
+        own=jnp.concatenate([dkh[j,:TOK] for j in range(4)]+[dvh[j,:TOK] for j in range(4)],axis=1)
+        both=(own+o[:,:2*HS]).astype(bf)
+        pack[...]=jnp.concatenate([dqh[j] for j in range(4)]+[both,jnp.zeros((TOK,HS),bf)],axis=1)
+        bsum_ref[z]=jnp.sum(pack[...].astype(f32),axis=0,keepdims=True)
+        pl.when(z>=2)(lambda: store(z-2).wait())
+        def tile(i,_):
+            cols=pl.ds(pl.multiple_of(i*384,384),384)
+            gx_ref[:,cols]+=dg(pack[...],w[k2,cols,:],1,1)
+            d1=dg(xt[cols],pack[:,:896],1,0)
+            d2=dg(gt[cols],att_ref[z],1,0)
+            dbuf[k2,cols,:AT0]=d1[:,:AT0].astype(bf)
+            dbuf[k2,cols,AT0:896]=(d1[:,AT0:]+d2[:,:128]).astype(bf)
+            dbuf[k2,cols,896:]=d2[:,128:].astype(bf)
+            return 0
+        lax.fori_loop(0,3,tile,0)
+        store(z).start()
+        return 0
+    lax.fori_loop(0,4,chunk,0)
+    store(2).wait(); store(3).wait()
+    for z in range(4): send(z).wait_send()
+
+def att_bwd(x,gb,g0,qkv,kvo,att,lse):
+    D=pltpu.SemaphoreType.DMA; M=pltpu.VMEM
+    return pl.pallas_call(att_bwd_kernel,name="att_bwd",
+      out_shape=(S((COLS,4*COLS),bf),S((TOK,COLS),f32),S((4,1,COLS),f32)),
+      in_specs=[VM,VM,HB,VM,VM,VM,VM],out_specs=(HB,VM,VM),
+      scratch_shapes=[M((2,COLS,COLS),bf),M((4,TOK,HEAD_DIM),bf),M((4,2*TOK,HEAD_DIM),bf),M((4,2*TOK,HEAD_DIM),bf),M((4,TOK,HEAD_DIM),bf),
+         M((4,TOK,HEAD_DIM),bf),M((4,2*TOK,HEAD_DIM),f32),M((4,2*TOK,HEAD_DIM),f32),M((4,TOK,KVW),bf),M((4,TOK,KVW),bf),M((TOK,COLS),bf),M((COLS,TOK),bf),M((COLS,TOK),bf),M((2,COLS,COLS),bf),
+         D((2,)),D((4,)),D((4,)),D((2,))],
+      compiler_params=pltpu.CompilerParams(collective_id=4,has_side_effects=True,vmem_limit_bytes=58*2**20))(x,gb,g0,qkv,kvo,att,lse)
+
+class Scatter:
+    def __init__(self, net, tensors, cc, d, rc, acc, tmp, far_in, near_in, line_in, out, send, core_sem, load_sem, tmp_sem, far_sem, near_sem, line_sem):
+        self.__dict__.update(locals()); self.count=0; self.started=[]; self.pending=[]
+        y,x=net.y,net.x
+        self.far_dev=net.yn if cc==0 else net.xn
+        self.near_dev=net.xn if cc==0 else net.yn
+    def place(self, far, near):
+        return (far,near) if self.cc==0 else (near,far)
+    def mine(self):
+        return (self.net.y,self.net.x) if self.cc==0 else (self.net.x,self.net.y)
+    def remote(self, src, dst, dev, recv, cond=None):
+        cp=pltpu.make_async_remote_copy(src_ref=src,dst_ref=dst,send_sem=self.send.at[self.count],recv_sem=recv,device_id=dev,device_id_type=MESH)
+        self.count+=1
+        if cond is None: cp.start()
+        else: pl.when(cond)(cp.start)
+        self.started.append((cond,cp))
+    def slots(self):
+        f,n=self.mine()
+        return [(ff,nn,z) for ff in (1-f,f) for nn in (1-n,n) for z in (0,3,1,2)]
+    def block(self,t,ff,nn,cc,z):
+        yy,xx=self.place(ff,nn)
+        row=(4*yy+2*xx+cc)*ROWS
+        return self.d[t].at[pl.ds(pl.multiple_of(row,16),ROWS),pl.ds(z*COLS,COLS)]
+    def begin(self,t):
+        for ff,nn,z in self.slots():
+            yy,xx=self.place(ff,nn)
+            self.remote(self.block(t,ff,nn,1-self.cc,z),self.rc.at[t,yy,xx,z],self.net.cn,self.core_sem.at[t,yy,xx,z])
+            pltpu.make_async_copy(self.block(t,ff,nn,self.cc,z),self.acc.at[t,yy,xx,z],self.load_sem.at[t,yy,xx,z]).start()
+    def add(self,a,b):
+        def one(i,_):
+            r=pl.ds(pl.multiple_of(i*16,16),16)
+            a[r]=(a[r].astype(jnp.float32)+b[r].astype(jnp.float32)).astype(a.dtype)
+            return 0
+        lax.fori_loop(0,ROWS//16,one,0)
+    def core_steps(self,t):
+        slots=self.slots()
+        n=len(slots)
+        def fetch(i):
+            ff,nn,z=slots[i]; yy,xx=self.place(ff,nn); r=self.rc.at[t,yy,xx,z]
+            pltpu.make_async_copy(r,r,self.core_sem.at[t,yy,xx,z]).wait()
+            pltpu.make_async_copy(r,self.tmp.at[i%2],self.tmp_sem.at[i%2]).start()
+        def step(i):
+            if i==0: fetch(0)
+            if i+1<n: fetch(i+1)
+            ff,nn,z=slots[i]; yy,xx=self.place(ff,nn)
+            a=self.acc.at[t,yy,xx,z]
+            pltpu.make_async_copy(a,a,self.load_sem.at[t,yy,xx,z]).wait()
+            pltpu.make_async_copy(self.rc.at[t,yy,xx,z],self.tmp.at[i%2],self.tmp_sem.at[i%2]).wait()
+            self.add(a,self.tmp.at[i%2])
+            if i<n//2: self.remote(a,self.far_in.at[t,nn,z],self.far_dev,self.far_sem.at[t,nn,z])
+        return [functools.partial(step,i) for i in range(n)]
+    def far_steps(self,t):
+        f,n=self.mine()
+        def step(nn,z,last):
+            yy,xx=self.place(f,nn); a=self.acc.at[t,yy,xx,z]; r=self.far_in.at[t,nn,z]
+            pltpu.make_async_copy(r,r,self.far_sem.at[t,nn,z]).wait()
+            self.add(a,r)
+            if not last: self.remote(a,self.near_in.at[t,z],self.near_dev,self.near_sem.at[t,z])
+        return [functools.partial(step,nn,z,last) for nn,last in ((1-n,False),(n,True)) for z in (0,3,1,2)]
+    def near_steps(self,t):
+        net=self.net; z=net.z
+        def step(zz):
+            a=self.acc.at[t,net.y,net.x,zz]; r=self.near_in.at[t,zz]
+            pltpu.make_async_copy(r,r,self.near_sem.at[t,zz]).wait()
+            self.add(a,r)
+            if zz==3:
+                pl.when(z==0)(lambda: self.line_send(t,3,1))
+            if zz==0:
+                pl.when(z==3)(lambda: self.line_send(t,0,0))
+        return [functools.partial(step,zz) for zz in (0,3,1,2)]
+    def line_send(self,t,zz,up):
+        pass
+    def line_steps(self,t):
+        net=self.net; z=net.z
+        up_dev=(net.y,net.x,net.c,lax.rem(z+1,4)); down_dev=(net.y,net.x,net.c,lax.rem(z+3,4))
+        def arrive(side,zz):
+            r=self.line_in.at[t,side,zz]
+            pltpu.make_async_copy(r,r,self.line_sem.at[t,side,zz]).wait()
+            return r
+        def up(zz):
+            a=self.acc.at[t,net.y,net.x,zz]
+            @pl.when(jnp.logical_and(z<zz,z>0))
+            def _(): self.add(a,arrive(0,zz))
+            self.remote(a,self.line_in.at[t,0,zz],up_dev,self.line_sem.at[t,0,zz],z<zz)
+        def down(zz):
+            a=self.acc.at[t,net.y,net.x,zz]
+            @pl.when(jnp.logical_and(z>zz,z<3))
+            def _(): self.add(a,arrive(1,zz))
+            self.remote(a,self.line_in.at[t,1,zz],down_dev,self.line_sem.at[t,1,zz],z>zz)
+        def last():
+            a=self.acc.at[t,net.y,net.x,z]
+            pl.when(z>0)(lambda: arrive(0,z) and None)
+            pl.when(z<3)(lambda: arrive(1,z) and None)
+            below=self.line_in.at[t,0,z]; above=self.line_in.at[t,1,z]
+            def one(i,_):
+                r=pl.ds(pl.multiple_of(i*16,16),16)
+                v=a[r].astype(jnp.float32)
+                v=v+jnp.where(z>0,below[r].astype(jnp.float32),0.0)
+                v=v+jnp.where(z<3,above[r].astype(jnp.float32),0.0)
+                self.out[t,r]=v
+                return 0
+            lax.fori_loop(0,ROWS//16,one,0)
+        return [functools.partial(up,3),functools.partial(down,0),functools.partial(up,2),functools.partial(down,1),functools.partial(up,1),functools.partial(down,2),last]
+    def finish(self):
+        for cond,cp in self.started:
+            if cond is None: cp.wait_send()
+            else: pl.when(cond)(cp.wait_send)
+
+def row_copies(net, pairs, send, recv):
+    y,x,c,z=net.y,net.x,net.c,net.z
+    dc=lax.div(z,2)
+    def each(start):
+        for a,(src,dst) in enumerate(pairs):
+            for k in range(2):
+                dz=2*c+k
+                here=jnp.logical_and(dc==c,dz==z)
+                rows=src.at[pl.ds(k*256,256)]; image=dst.at[lax.rem(z,2)]
+                cp=pltpu.make_async_remote_copy(src_ref=rows,dst_ref=image,send_sem=send.at[a,k],recv_sem=recv.at[a,lax.rem(z,2)],device_id=(y,x,dc,dz),device_id_type=MESH)
+                lc=pltpu.make_async_copy(rows,image,recv.at[a,lax.rem(z,2)])
+                pl.when(jnp.logical_not(here))(cp.start if start else cp.wait_send)
+                if start: pl.when(here)(lc.start)
+    def arrivals():
+        for a,(src,dst) in enumerate(pairs):
+            for i in range(2):
+                pltpu.make_async_copy(dst.at[i],dst.at[i],recv.at[a,i]).wait()
+    return each,arrivals
+
+def scatter_kernel(T, d0, d1, d2, r0, r1, out, rc, b0, b1, acc, tmp, far_in, near_in, line_in, row_send, row_recv, *sems):
+    net=Net(); enter(net,True)
+    each,arrivals=row_copies(net,((r0,b0),(r1,b1)),row_send,row_recv)
+    each(True)
+    def flow(cc):
+        s=Scatter(net,T,cc,[d0,d1,d2],rc,acc,tmp,far_in,near_in,line_in,out,*sems)
+        for t in range(T): s.begin(t)
+        for t in range(T):
+            for f in s.core_steps(t): f()
+            if t>0:
+                for f in s.far_steps(t-1): f()
+            if t>1:
+                for f in s.near_steps(t-2)+s.line_steps(t-2): f()
+        for f in s.far_steps(T-1): f()
+        for t in range(max(T-2,0),T):
+            for f in s.near_steps(t)+s.line_steps(t): f()
+        s.finish()
+    pl.when(net.c==0)(lambda: flow(0))
+    pl.when(net.c==1)(lambda: flow(1))
+    arrivals(); each(False)
+
+def scatter(d0,d1,d2,r0,r1):
+    T=3; bf=jnp.bfloat16
+    D=pltpu.SemaphoreType.DMA
+    hbm=pl.BlockSpec(memory_space=pl.ANY)
+    B=(ROWS,COLS)
+    out=pl.pallas_call(functools.partial(scatter_kernel,T),name="scatter",
+      out_shape=(jax.ShapeDtypeStruct((T,)+B,jnp.float32),jax.ShapeDtypeStruct((T,2,2,4)+B,bf))+(jax.ShapeDtypeStruct((2,256,COLS),bf),)*2,
+      in_specs=[hbm]*5,out_specs=(pl.BlockSpec(memory_space=pltpu.VMEM),hbm,hbm,hbm),
+      scratch_shapes=[pltpu.VMEM((T,2,2,4)+B,bf),pltpu.VMEM((2,)+B,bf),pltpu.VMEM((T,2,4)+B,bf),pltpu.VMEM((T,4)+B,bf),pltpu.VMEM((T,2,4)+B,bf),
+         D((2,2)),D((2,2)),D((T*36,)),D((T,2,2,4)),D((T,2,2,4)),D((2,)),D((T,2,4)),D((T,4)),D((T,2,4))],
+      compiler_params=pltpu.CompilerParams(collective_id=2,has_side_effects=True,vmem_limit_bytes=58*2**20))(d0,d1,d2,r0,r1)
+    return out[0],out[2],out[3]
+
+def modulate(values, shift, scale):
+    average = jnp.mean(values, axis=-1, keepdims=True)
+    centred = values - average
+    spread = jnp.mean(centred * centred, axis=-1, keepdims=True)
+    return centred * lax.rsqrt(spread + epsilon) * (1.0 + scale) + shift
+
+
+def one_image_per_chip(
+    tokens, conditioning, cotangent, query_weight, key_weight, value_weight, out_weight, up_weight,
+    down_weight, ada_weight, query_bias, value_bias, out_bias, up_bias, down_bias, ada_bias, threshold,
+):
+    y, x, c, z = (lax.axis_index(a) for a in AXES)
+    plane = 2 * y + x
+    batch = 4 * y + 2 * x + c
+    first = jnp.concatenate([query_weight, key_weight, value_weight, out_weight.T], axis=1)
+    shard = jnp.stack([first, up_weight, down_weight.T])
+    full0, full1, full2, own_tokens, own_cotangent = gather(shard, tokens, cotangent)
+
+    lifted = jax.nn.silu(conditioning).astype(bf)
+    every_lifted = lax.all_gather(lifted, ("y", "x", "core"), axis=0, tiled=True)
+    lifted_rows = lax.dynamic_slice(every_lifted, (0, batch * ROWS), (16, ROWS))
+    partial = product(lifted_rows, ada_weight)
+    columns = lax.psum(partial, ("y", "x", "core")) + ada_bias
+    four = lax.dynamic_slice(columns, (4 * plane, 0), (4, columns.shape[1]))
+    biases = jnp.concatenate([query_bias, value_bias, up_bias])[None]
+    by_z = lax.all_gather(jnp.concatenate([four, biases]), "z", axis=0)
+    vectors = lax.dynamic_slice(by_z, (0, z, 0), (4, 1, by_z.shape[2])).reshape(6, 1, COLS)
+    shift_attn, scale_attn, gate_attn, shift_mlp, scale_mlp, gate_mlp = vectors
+    all_bias = by_z[:, 4]
+    nothing = jnp.zeros((4, HS), f32)
+    bias0 = jnp.concatenate([all_bias[:, :HS], nothing, all_bias[:, HS : 2 * HS], nothing], axis=1)
+    full_up_bias = all_bias[:, 2 * HS :].reshape(1, 4 * COLS)
+
+    inputs = own_tokens.astype(f32)
+    normed_attn = modulate(inputs, shift_attn, scale_attn).astype(bf)
+    qkv, mate_kv, attended, totals, peak, branch_attn = att_fwd(normed_attn, full0, bias0[:, None])
+    branch_attn = branch_attn + out_bias
+    after_attn = inputs + gate_attn * branch_attn
+    normed_mlp = modulate(after_attn, shift_mlp, scale_mlp).astype(bf)
+    upward = product(normed_mlp, full1) + full_up_bias
+    active = jax.nn.gelu(upward, approximate=True).astype(bf)
+    branch_mlp = against(active, full2) + down_bias
+    block_out = (after_attn + gate_mlp * branch_mlp).astype(bf)
+
+    grad_out = own_cotangent.astype(f32)
+    grad_branch_mlp = (gate_mlp * grad_out).astype(bf)
+    grad_gate_mlp = jnp.sum(grad_out * branch_mlp, axis=0)
+    grad_down_bias = jnp.sum(grad_branch_mlp, axis=0, dtype=f32)
+    grad_down = inner_rows(grad_branch_mlp, active).astype(bf)
+    grad_active = product(grad_branch_mlp, full2)
+    _, gelu_pull = jax.vjp(partial_gelu, upward)
+    grad_upward = gelu_pull(grad_active)[0].astype(bf)
+    grad_up_bias = jnp.sum(grad_upward, axis=0, dtype=f32)
+    grad_up = inner_rows(normed_mlp, grad_upward).astype(bf)
+    grad_normed_mlp = against(grad_upward, full1)
+    _, mlp_pull = jax.vjp(modulate, after_attn, shift_mlp, scale_mlp)
+    grad_after, grad_shift_mlp, grad_scale_mlp = mlp_pull(grad_normed_mlp)
+    grad_after = grad_out + grad_after
+    grad_branch_attn = (gate_attn * grad_after).astype(bf)
+    grad_gate_attn = jnp.sum(grad_after * branch_attn, axis=0)
+    grad_out_bias = jnp.sum(grad_branch_attn, axis=0, dtype=f32)
+    grad_first, grad_normed_attn, bias_sums = att_bwd(
+        normed_attn, grad_branch_attn, full0, qkv, mate_kv, attended, totals
+    )
+    _, attn_pull = jax.vjp(modulate, inputs, shift_attn, scale_attn)
+    grad_inputs, grad_shift_attn, grad_scale_attn = attn_pull(grad_normed_attn)
+    grad_tokens = grad_after + grad_inputs
+    sums, block_rows, token_rows = scatter(
+        grad_first, grad_up, grad_down, block_out, grad_tokens.astype(bf)
+    )
+
+    own_terms = jnp.concatenate(
+        [
+            grad_shift_attn, grad_scale_attn, grad_gate_attn[None],
+            grad_shift_mlp, grad_scale_mlp, grad_gate_mlp[None],
+        ],
+        axis=0,
+    ).reshape(4, 6 * COLS // 4)
+    image_terms = lax.psum(own_terms, "core").astype(bf)
+    four_images = lax.all_gather(image_terms, "z", axis=0)
+    four_images = lax.dynamic_slice(four_images, (0, z, 0), (4, 1, image_terms.shape[1]))[:, 0]
+    grad_modulation = lax.all_gather(four_images, ("y", "x"), axis=0, tiled=True)
+    grad_ada_bias = jnp.sum(grad_modulation, axis=0, dtype=f32)
+    grad_ada_weight = inner_rows(lifted_rows, grad_modulation)
+    grad_lifted = lax.psum(against(grad_modulation, ada_weight), "z")
+    by_batch = lax.all_gather(grad_lifted, ("y", "x", "core"), axis=0)
+    own_lifted = lax.dynamic_slice(by_batch, (0, 2 * batch, 0), (8, 2, ROWS))
+    own_lifted = jnp.swapaxes(own_lifted, 0, 1).reshape(2, 8 * ROWS)
+    _, silu_pull = jax.vjp(jax.nn.silu, conditioning)
+    grad_conditioning = silu_pull(own_lifted)[0]
+
+    bias_vector = jnp.concatenate(
+        [bias_sums.reshape(-1), grad_up_bias, grad_out_bias, grad_down_bias]
+    )
+    bias_total = lax.psum(bias_vector, AXES)
+    first_bias = lax.dynamic_slice(bias_total, (z * COLS,), (COLS,))
+    grad_query_bias = first_bias[:HS]
+    grad_value_bias = first_bias[2 * HS : 3 * HS]
+    grad_up_bias = lax.dynamic_slice(bias_total, ((4 + z) * COLS,), (COLS,))
+    grad_out_bias = bias_total[8 * COLS : 9 * COLS]
+    grad_down_bias = bias_total[9 * COLS :]
+
+    peaks = lax.pmax(peak[:, 0, 0], AXES)
+    limit = threshold[0]
+    factor = jnp.sqrt(limit / jnp.maximum(lax.dynamic_slice(peaks, (4 * z,), (4,)), limit))
+    column_factor = jnp.repeat(factor, HEAD_DIM)
+    query_clipped = (query_weight.astype(f32) * column_factor).astype(bf)
+    key_clipped = (key_weight.astype(f32) * column_factor).astype(bf)
+    return (
+        block_rows,
+        token_rows.astype(f32),
+        grad_conditioning,
+        sums[0, :, :HS],
+        sums[0, :, HS : 2 * HS],
+        sums[0, :, 2 * HS : 3 * HS],
+        sums[0, :, 3 * HS :].T,
+        sums[1],
+        sums[2].T,
+        grad_ada_weight,
+        grad_query_bias,
+        grad_value_bias,
+        grad_out_bias,
+        grad_up_bias,
+        grad_down_bias,
+        grad_ada_bias,
+        query_clipped,
+        key_clipped,
+        query_bias * column_factor,
+    )
+
+
 def solution(mesh):
+    if dict(mesh.shape) == {"dp": 8, "tensor": 4}:
+        mesh = Mesh(mesh.devices.reshape(2, 2, 2, 4), AXES)
+        split, heads, body = ("y", "x", "core"), "z", one_image_per_chip
+    else:
+        split, heads, body = "dp", "tensor", local
+    weight, turned, bias = P(split, heads), P(heads, split), P(heads)
+    rows = P(split, heads, None)
     in_specs = (
-        P("dp", "tensor", None),
-        P("dp", None),
-        P("dp", "tensor", None),
-        P("dp", "tensor"),
-        P("dp", "tensor"),
-        P("dp", "tensor"),
-        P("tensor", "dp"),
-        P("dp", "tensor"),
-        P("tensor", "dp"),
-        P("dp", "tensor"),
-        P("tensor"),
-        P("tensor"),
-        P(),
-        P("tensor"),
-        P(),
-        P("tensor"),
-        P(),
+        rows, P(split, None), rows, weight, weight, weight, turned, weight, turned, weight,
+        bias, bias, P(), bias, P(), bias, P(),
     )
     out_specs = (
-        P("dp", "tensor", None),
-        P("dp", "tensor", None),
-        P("dp", None),
-        P("dp", "tensor"),
-        P("dp", "tensor"),
-        P("dp", "tensor"),
-        P("tensor", "dp"),
-        P("dp", "tensor"),
-        P("tensor", "dp"),
-        P("dp", "tensor"),
-        P("tensor"),
-        P("tensor"),
-        P(),
-        P("tensor"),
-        P(),
-        P("tensor"),
-        P("dp", "tensor"),
-        P("dp", "tensor"),
-        P("tensor"),
-    )
-    return jax.shard_map(local, mesh=mesh, in_specs=in_specs, out_specs=out_specs, check_vma=False)
+        rows, rows, P(split, None), weight, weight, weight, turned, weight, turned, weight,
+        bias, bias, P(), bias, P(), bias, weight, weight, bias,
+    )
+    return jax.shard_map(body, mesh=mesh, in_specs=in_specs, out_specs=out_specs, check_vma=False)

time: 1800 us -> 769 us (0.43)
  waiting for transfers between devices: 1340 us -> 0.04 us
  Pallas kernels: 0 us -> 468 us
  matrix products: 211 us -> 80.3 us
  blocking collectives: 103 us -> 160 us
  other arithmetic: 72.6 us -> 23.1 us
  local copies, waits for them, and re-layouts: 52.8 us -> 11.9 us
    reduce_scatter x11 -> x0, waiting for transfers between devices: 930 us -> none  [the longest x2 316 us: fold_rows(): return lax.psum_scatter(values, 'tensor', scatter_dimension=1, tiled=True)]
    pallas_call x0 -> x4, Pallas kernels: none -> 468 us  [the longest x1 186 us: scatter(): pl.pallas_call(functools.partial(scatter_kernel, T), name='scatter', out_...]
    all_gather x7 -> x0, waiting for transfers between devices: 394 us -> none  [the longest x2 177 us: spread_grads(): return lax.all_gather(values, 'tensor', axis=1, tiled=True)]
    dot_general x28 -> x0, matrix products: 58.9 us -> none  [the longest x4 17.9 us: attend_back(): jnp.einsum('qhe,khe->hqk', grad_block, values_img, preferred_element_type...]
    dot_general x7 -> x3, matrix products: 56.4 us -> 21.5 us  [inner_rows(): lax.dot_general(left, right, (((0,), (0,)), ((), ())), preferred_element_...]
    pmax x1, blocking collectives: 12.7 us -> 47.2 us  [one_image_per_chip(): peaks = lax.pmax(peak[:, 0, 0], AXES)]
    dot_general x7 -> x3, matrix products: 55.5 us -> 28.9 us  [product(): return jnp.dot(left, right, preferred_element_type=jnp.float32)]
    psum x2 -> x3, blocking collectives: 33.1 us -> 58.2 us  [the longest x1 39.2 us: one_image_per_chip(): bias_total = lax.psum(bias_vector, AXES)]
  transfers between devices with their start and end apart: 19 -> 1, of which waited for: 18 -> 0; matrix products, arithmetic and copies ran while one was open for 6% -> 1% of each run, Pallas kernels for 0% -> 21%
where the time goes in v1:
time: 769 us; the launch traced here: 759 us
  Pallas kernels  468 us (61%)
  blocking collectives  160 us (21%)
  matrix products  80.3 us (10%)
  other arithmetic  23.1 us (3%)
  between operations  15.4 us (2%)
  local copies, waits for them, and re-layouts  11.9 us (2%)
    pallas_call x1, Pallas kernels, scatter(): pl.pallas_call(functools.partial(scatter_kernel, T), name='scatter', out_...  186 us
    pallas_call x1, Pallas kernels, gather(): pl.pallas_call(functools.partial(gather_kernel, T), out_shape=(jax.ShapeD...  159 us
    pallas_call x1, Pallas kernels, att_bwd(): pl.pallas_call(att_bwd_kernel, name='att_bwd', out_shape=(S((COLS, 4 * CO...  74.7 us
    pallas_call x1, Pallas kernels, att_fwd(): pl.pallas_call(att_fwd_kernel, name='att_fwd', out_shape=(S((4, TOK, COLS...  48.8 us
    pmax x1, blocking collectives, one_image_per_chip(): peaks = lax.pmax(peak[:, 0, 0], AXES)  47.2 us
    psum x1, blocking collectives, one_image_per_chip(): bias_total = lax.psum(bias_vector, AXES)  39.2 us
    dot_general x3, matrix products, against(): lax.dot_general(left, right, (((1,), (1,)), ((), ())), preferred_element_...  29.9 us
    dot_general x3, matrix products, product(): return jnp.dot(left, right, preferred_element_type=jnp.float32)  28.9 us
  transfers between devices with their start and end apart: 1, of which 0 were waited for; matrix products, arithmetic and copies ran while one was open for 1% of the time, Pallas kernels for 21%

profile of v1, /device:TPU:28, one launch (start us, length us, event | category | flops | bytes accessed | tf_op | source)
XLA Modules:
  0.0 759.1 jit_solution(5593165512813795726)
XLA Ops:
  8.0 9.1 %all-gather.3 = bf16[8,2,1152]{2,1,0:T(2,128)(2,1)S(1)} all-gather(bf16[1,2,1152]{2,1,0:T(2,128)(2,1)S(1)} %fusion.33), channel_id=1, replica_groups=mesh['y'=2,'x'=2,'core'=2,'z'=4] {'y','x','core'}, dimensions={0}, use_global_device_ids=true | all-gather | bytes 41472 | tf_op jit(solution)/shard_map/all_gather | solution.py:794
  19.4 2.2 pad_maximum_fusion.s_ref
  21.5 159.0 %shard_map.312 = (bf16[1152,4608]{1,0:T(8,128)(2,1)}, bf16[1152,4608]{1,0:T(8,128)(2,1)}, bf16[1152,4608]{1,0:T(8,128)(2,1)}, bf16[512,1152]{1,0:T(8,128)(2,1)}, bf16[512,1152]{1,0:T(8,128)(2,1)}) custom-call(bf16[3,144,1152]{2,1,0:T(8,128)(2,1)} %pad_maximum_fusion.s_ref, bf16[2,256,1152]{2,1,0:T(8,128)(2,1)} %tok_ref.1, bf16[2,256,1152]{2,1,0:T(8,128)(2,1)} %cot_ref.1), custom_call_target="tpu_custom_call" | custom-call | tf_op jit(solution)/shard_map/pallas_call | solution.py:466
  180.6 1.6 convert_reduce_fusion.1
  182.2 1.7 fusion.16
  185.6 14.3 %all-gather.4 = f32[4,5,1728]{2,1,0:T(8,128)S(1)} all-gather(f32[1,5,1728]{2,1,0:T(8,128)S(1)} %maximum_bitcast_fusion), channel_id=2, replica_groups=mesh['y'=2,'x'=2,'core'=2,'z'=4] {'z'}, dimensions={0}, use_global_device_ids=true | all-gather | bytes 172800 | tf_op jit(solution)/shard_map/all_gather | solution.py:800
  201.2 1.5 fusion.14.x_ref
  202.7 48.8 %att_fwd.1 = (bf16[4,512,1152]{2,1,0:T(8,128)(2,1)}, bf16[4,512,640]{2,1,0:T(8,128)(2,1)}, bf16[4,512,384]{2,1,0:T(8,128)(2,1)}, f32[16,1,512]{2,1,0:T(1,128)}, ...) custom-call(bf16[512,1152]{1,0:T(8,128)(2,1)} %fusion.14.x_ref, bf16[1152,4608]{1,0:T(8,128)(2,1)} %get-tuple-element.39.g0_ref, ...), custom_call_target="tpu_custom_call" | custom-call | tf_op jit(solution)/shard_map/att_fwd/pallas_call | solution.py:537
  251.5 2.1 fusion.45
  253.7 1.4 copy-done.2
  255.5 12.3 %fusion.43 = f32[512,4608]{1,0:T(8,128)} fusion(bf16[1152,4608]{1,0:T(8,128)(2,1)} %get-tuple-element.41, f32[512,1152]{1,0:T(8,128)} %copy-done.2, f32[1152]{0:T(1024)S(1)} %get-tuple-element.63, f32[1152]{0:T(1024)S(1)} %get-tuple-element.64, f32[512]{0:T(512)S(1)} %fusion.37, f32[512]{0:T(512)S(1)} %broadcast_multiply_fusion), kind=kOutput, calls=%fused_computation.102 | convolution fusion | flops 5438767104 | bytes 22426624 | tf_op jit(solution)/shard_map/dot_general | solution.py:23
  267.8 15.7 %convert_reduce_fusion = (f32[4608]{0:T(1024)S(1)}, bf16[512,4608]{1,0:T(8,128)(2,1)S(1)}) fusion(f32[512,4608]{1,0:T(8,128)} %fusion.43, f32[4608]{0:T(1024)S(1)} %add.193, bf16[1152,4608]{1,0:T(8,128)(2,1)} %get-tuple-element.38, bf16[512,1152]{1,0:T(8,128)(2,1)S(1)} %copy-done.8, f32[1152]{0:T(1024)S(1)} %get-tuple-element.62), kind=kOutput, calls=%fused_computation.11 | convolution fusion | flops 5491846656 | bytes 25993728 | tf_op jit(solution)/shard_map/dot_general | solution.py:23
  283.5 12.3 %multiply_reduce_fusion = (f32[1152]{0:T(1024)S(1)}, f32[512]{0:T(512)S(1)}, f32[1152]{0:T(1024)S(1)}, f32[512,1152]{1,0:T(8,128)S(1)}) fusion(f32[512,1152]{1,0:T(8,128)S(1)} %copy-done.3, f32[512]{0:T(512)S(1)} %fusion.37, f32[512]{0:T(512)S(1)} %broadcast_multiply_fusion, f32[1152]{0:T(1024)S(1)} %get-tuple-element.64, ...), kind=kOutput, calls=%fused_computation.37 | convolution fusion | flops 5440534016 | bytes 20073984 | tf_op jit(solution)/shard_map/dot_general | solution.py:33
  295.8 2.1 fusion.44
  297.9 17.4 %convert_reduce_fusion.2 = (f32[1152]{0:T(1024)S(1)}, f32[1152]{0:T(1024)S(1)}, f32[1152]{0:T(1024)S(1)}, f32[1152]{0:T(1024)S(1)}, bf16[512,1152]{1,0:T(8,128)(2,1)}, /*index=5*/bf16[512,1152]{1,0:T(8,128)(2,1)}) fusion(bf16[512,1152]{1,0:T(8,128)(2,1)S(1)} %copy-done.8, f32[1152]{0:T(1024)S(1)} %get-tuple-element.62, f32[512,1152]{1,0:T(8,128)} %get-tuple-element.40, ...), kind=kOutput, calls=%fused_computation.35 | convolution fusion | flops 5471203328 | bytes 30728192 | tf_op jit(solution)/shard_map/dot_general | solution.py:33
  315.3 74.7 %att_bwd.1 = (bf16[1152,4608]{1,0:T(8,128)(2,1)}, f32[512,1152]{1,0:T(8,128)}, f32[4,1,1152]{2,1,0:T(1,128)}) custom-call(bf16[512,1152]{1,0:T(8,128)(2,1)} %fusion.14.x_ref, bf16[512,1152]{1,0:T(8,128)(2,1)} %get-tuple-element.75.gb_ref, bf16[1152,4608]{1,0:T(8,128)(2,1)} %get-tuple-element.39.g0_ref, bf16[4,512,1152]{2,1,0:T(8,128)(2,1)} %get-tuple-element.42.qkv_ref, ...), custom_call_target="tpu_custom_call" | custom-call | tf_op jit(solution)/shard_map/att_bwd/pallas_call | solution.py:606
  390.0 2.3 fusion.17
  393.7 3.9 psum.29
  397.6 13.1 %all-gather.5 = bf16[4,4,1728]{2,1,0:T(4,128)(2,1)S(1)} all-gather(bf16[1,4,1728]{2,1,0:T(4,128)(2,1)S(1)} %bitcast.58), channel_id=3, replica_groups=mesh['y'=2,'x'=2,'core'=2,'z'=4] {'z'}, dimensions={0}, use_global_device_ids=true | all-gather | bytes 69120 | tf_op jit(solution)/shard_map/all_gather | solution.py:854
  410.8 8.9 %all-gather.2 = bf16[16,1,1728]{2,1,0:T(2,128)(2,1)S(1)} all-gather(bf16[4,1,1728]{2,1,0:T(2,128)(2,1)S(1)} %constant_dynamic-slice_fusion), channel_id=4, replica_groups=mesh['y'=2,'x'=2,'core'=2,'z'=4] {'y','x'}, dimensions={0}, use_global_device_ids=true | all-gather | bytes 69120 | tf_op jit(solution)/shard_map/all_gather | solution.py:856
  419.7 1.4 fusion.25
  421.3 11.3 %convolution_convert_fusion.d2 = bf16[1152,4608]{1,0:T(8,128)(2,1)} fusion(bf16[512,1152]{1,0:T(8,128)(2,1)S(1)} %copy-done.8, f32[1152]{0:T(1024)S(1)} %get-tuple-element.62, f32[512,4608]{1,0:T(8,128)} %fusion.43, f32[4608]{0:T(1024)S(1)} %add.193), kind=kOutput, calls=%fused_computation | convolution fusion | flops 5466488832 | bytes 21256704 | tf_op jit(solution)/shard_map/dot_general | solution.py:27
  432.6 8.8 %convolution_convert_fusion.1.d1 = bf16[1152,4608]{1,0:T(8,128)(2,1)} fusion(bf16[512,4608]{1,0:T(8,128)(2,1)S(1)} %bitcast.60, f32[512,1152]{1,0:T(8,128)S(1)} %copy-done.4, f32[1152]{0:T(1024)S(1)} %get-tuple-element.63, f32[1152]{0:T(1024)S(1)} %get-tuple-element.64, f32[512]{0:T(512)S(1)} %fusion.37, f32[512]{0:T(512)S(1)} %broadcast_multiply_fusion), kind=kOutput, calls=%fused_computation.1 | convolution fusion | flops 5444075520 | bytes 17708032 | tf_op jit(solution)/shard_map/dot_general | solution.py:27
  441.4 2.0 add_convert_fusion.r1
  443.4 185.6 %scatter.1 = (f32[3,144,1152]{2,1,0:T(8,128)}, bf16[3,2,2,4,144,1152]{5,4,3,2,1,0:T(8,128)(2,1)}, bf16[2,256,1152]{2,1,0:T(8,128)(2,1)}, bf16[2,256,1152]{2,1,0:T(8,128)(2,1)}) custom-call(bf16[1152,4608]{1,0:T(8,128)(2,1)} %get-tuple-element.46.d0, bf16[1152,4608]{1,0:T(8,128)(2,1)} %convolution_convert_fusion.1.d1, ...), custom_call_target="tpu_custom_call" | custom-call | tf_op jit(solution)/shard_map/scatter/pallas_call | solution.py:767
  629.1 2.5 slice_bitcast_fusion
  631.6 2.3 slice_bitcast_fusion.2
  634.8 47.2 %pmax.7 = f32[16]{0:T(128)S(1)} all-reduce(f32[16]{0:T(128)S(1)} %slice_reduce_fusion), channel_id=1, replica_groups=mesh['y'=2,'x'=2,'core'=2,'z'=4] {'y','x','core','z'}, use_global_device_ids=true, to_apply=%region_22.23 | all-reduce | flops 16 | bytes 128 | tf_op jit(solution)/shard_map/pmax | solution.py:877
  683.6 39.2 %psum.31 = f32[11520]{0:T(1024)S(1)} all-reduce(f32[11520]{0:T(1024)S(1)} %pad_maximum_fusion.1), channel_id=1, replica_groups=mesh['y'=2,'x'=2,'core'=2,'z'=4] {'y','x','core','z'}, use_global_device_ids=true, to_apply=%region_20.21 | all-reduce | flops 11520 | bytes 92160 | tf_op jit(solution)/shard_map/psum | solution.py:869
  724.1 15.1 %psum.30 = f32[1,16,144]{2,1,0:T(8,128)S(1)} all-reduce(f32[1,16,144]{2,1,0:T(8,128)S(1)} %convolution_bitcast_fusion), channel_id=1, replica_groups=mesh['y'=2,'x'=2,'core'=2,'z'=4] {'z'}, use_global_device_ids=true, to_apply=%region_16.17 | all-reduce | flops 2304 | bytes 18432 | tf_op jit(solution)/shard_map/psum | solution.py:859
  739.3 9.4 %all_gather.31 = f32[8,16,144]{2,1,0:T(8,128)S(1)} all-gather(f32[1,16,144]{2,1,0:T(8,128)S(1)} %psum.30), channel_id=1, replica_groups=mesh['y'=2,'x'=2,'core'=2,'z'=4] {'y','x','core'}, dimensions={0}, use_global_device_ids=true | all-gather | bytes 82944 | tf_op jit(solution)/shard_map/all_gather | solution.py:860
  749.5 1.6 convert_element_type.82
  (108 shorter events, 12.9 us)
Async XLA Ops:
  7.2 9.9 %copy-start = (bf16[144,1728]{1,0:T(8,128)(2,1)S(1)}, bf16[144,1728]{1,0:T(8,128)(2,1)}, u32[]{:S(2)}) copy-start(bf16[144,1728]{1,0:T(8,128)(2,1)} %param.26) | copy-start | bytes 1492996
  7.2 177.5 %all-reduce.2.cloned.1.call-start = ((), (), s32[]{:S(2)}) async-start(), calls=%async_computation | async-start | bytes 229376 | tf_op jit(solution)/shard_map/psum | solution.py:797
  21.5 162.4 %copy-start.16 = (f32[288]{0:T(512)S(1)}, f32[288]{0:T(512)}, u32[]{:S(2)}) copy-start(f32[288]{0:T(512)} %param.27) | copy-start | bytes 3460
  21.5 162.4 %copy-start.17 = (f32[1152]{0:T(1024)S(1)}, f32[1152]{0:T(1024)}, u32[]{:S(2)}) copy-start(f32[1152]{0:T(1024)} %param.30) | copy-start | bytes 13828
  21.5 162.4 %copy-start.20 = (f32[288]{0:T(512)S(1)}, f32[288]{0:T(512)}, u32[]{:S(2)}) copy-start(f32[288]{0:T(512)} %param.28) | copy-start | bytes 3460
  21.5 163.2 %copy-start.19 = (f32[1728]{0:T(1024)S(1)}, f32[1728]{0:T(1024)}, u32[]{:S(2)}) copy-start(f32[1728]{0:T(1024)} %param.32) | copy-start | bytes 20740
  180.6 20.6 %copy-start.1 = (bf16[512,1152]{1,0:T(8,128)(2,1)S(1)}, bf16[512,1152]{1,0:T(8,128)(2,1)}, u32[]{:S(2)}) copy-start(bf16[512,1152]{1,0:T(8,128)(2,1)} %get-tuple-element.36) | copy-start | bytes 3538948
  202.7 48.9 %copy-start.15 = (f32[1152]{0:T(1024)S(1)}, f32[1152]{0:T(1024)}, u32[]{:S(2)}) copy-start(f32[1152]{0:T(1024)} %param.29) | copy-start | bytes 13828
  253.7 1.4 copy-start.2
  255.5 12.3 %copy-start.8 = (bf16[512,1152]{1,0:T(8,128)(2,1)S(1)}, bf16[512,1152]{1,0:T(8,128)(2,1)}, u32[]{:S(2)}) copy-start(bf16[512,1152]{1,0:T(8,128)(2,1)} %get-tuple-element.37) | copy-start | bytes 3538948
  267.8 15.7 %copy-start.3 = (f32[512,1152]{1,0:T(8,128)S(1)}, f32[512,1152]{1,0:T(8,128)}, u32[]{:S(2)}) copy-start(f32[512,1152]{1,0:T(8,128)} %copy-done.2) | copy-start | bytes 7077892
  283.5 12.3 %copy-start.22 = (bf16[512,4608]{1,0:T(8,128)(2,1)}, bf16[512,4608]{1,0:T(8,128)(2,1)S(1)}, u32[]{:S(2)}) copy-start(bf16[512,4608]{1,0:T(8,128)(2,1)S(1)} %get-tuple-element.96) | copy-start | bytes 14155780
  295.8 2.1 copy-start.21
  390.0 2.4 copy-start.5
  419.7 12.9 %slice-start = ((s8[4718592]{0:T(1024)(128)(4,1)}), s8[4194304]{0:T(1024)(128)(4,1)S(1)}, s32[]{:S(2)}) async-start(s8[4718592]{0:T(1024)(128)(4,1)} %bitcast.59), calls=%async_computation.1 | async-start | bytes 8388608
  421.2 11.3 %copy-start.4 = (f32[512,1152]{1,0:T(8,128)S(1)}, f32[512,1152]{1,0:T(8,128)}, u32[]{:S(2)}) copy-start(f32[512,1152]{1,0:T(8,128)} %copy-done.2) | copy-start | bytes 7077892
  421.2 11.3 %slice-start.1 = ((s8[4718592]{0:T(1024)(128)(4,1)}), s8[524288]{0:T(1024)(128)(4,1)S(1)}, s32[]{:S(2)}) async-start(s8[4718592]{0:T(1024)(128)(4,1)} %bitcast.59), calls=%async_computation.2 | async-start | bytes 1048576
  432.6 8.9 %copy-start.6 = (f32[512,1152]{1,0:T(8,128)S(1)}, f32[512,1152]{1,0:T(8,128)}, u32[]{:S(2)}) copy-start(f32[512,1152]{1,0:T(8,128)} %get-tuple-element.47) | copy-start | bytes 7077892
  432.6 8.9 %copy-start.7 = (f32[512,1152]{1,0:T(8,128)S(1)}, f32[512,1152]{1,0:T(8,128)}, u32[]{:S(2)}) copy-start(f32[512,1152]{1,0:T(8,128)} %get-tuple-element.71) | copy-start | bytes 7077892
  629.0 4.9 copy-start.18
  629.0 53.2 %copy-start.11 = (bf16[144,288]{1,0:T(8,128)(2,1)S(1)}, bf16[144,288]{1,0:T(8,128)(2,1)}, u32[]{:S(2)}) copy-start(bf16[144,288]{1,0:T(8,128)(2,1)} %param.20) | copy-start | bytes 248836
  629.0 53.2 %copy-start.12 = (bf16[144,288]{1,0:T(8,128)(2,1)S(1)}, bf16[144,288]{1,0:T(8,128)(2,1)}, u32[]{:S(2)}) copy-start(bf16[144,288]{1,0:T(8,128)(2,1)} %param.21) | copy-start | bytes 248836
  629.0 54.5 %copy-start.14 = (f32[4,1,1152]{2,1,0:T(1,128)S(1)}, f32[4,1,1152]{2,1,0:T(1,128)}, u32[]{:S(2)}) copy-start(f32[4,1,1152]{2,1,0:T(1,128)} %get-tuple-element.51) | copy-start | bytes 55300
  629.1 119.8 %copy-start.13 = (f32[2,1152]{1,0:T(2,128)S(1)}, f32[2,1152]{1,0:T(2,128)}, u32[]{:S(2)}) copy-start(f32[2,1152]{1,0:T(2,128)} %param.18) | copy-start | bytes 27652
  629.1 120.4 %copy-start.9 = (bf16[2,256,1152]{2,1,0:T(8,128)(2,1)S(1)}, bf16[2,256,1152]{2,1,0:T(8,128)(2,1)}, u32[]{:S(2)}) copy-start(bf16[2,256,1152]{2,1,0:T(8,128)(2,1)} %get-tuple-element.49) | copy-start | bytes 3538948
  634.8 116.3 %copy-start.10 = (bf16[2,256,1152]{2,1,0:T(8,128)(2,1)S(1)}, bf16[2,256,1152]{2,1,0:T(8,128)(2,1)}, u32[]{:S(2)}) copy-start(bf16[2,256,1152]{2,1,0:T(8,128)(2,1)} %get-tuple-element.116) | copy-start | bytes 3538948
Sparse Core Ops, SparseCore 0:
  18.2 53.0 all-reduce.1

commit v2 on v1

--- a/solution.py
+++ b/solution.py
@@ -327,147 +327,6 @@
     )
 
 
-MESH = pl.DeviceIdType.MESH
-AXES=("y","x","core","z")
-
-class Net:
-    def __init__(self):
-        self.y,self.x,self.c,self.z=(lax.axis_index(a) for a in AXES)
-        y,x,c,z=self.y,self.x,self.c,self.z
-        self.zp=lax.rem(z+1,4); self.zm=lax.rem(z+3,4); self.zo=lax.rem(z+2,4)
-        self.xn=(y,1-x,c,z); self.yn=(1-y,x,c,z); self.cn=(y,x,1-c,z)
-        self.zpn=(y,x,c,self.zp); self.zmn=(y,x,c,self.zm)
-
-def enter(net, column):
-    bar=pltpu.get_barrier_semaphore()
-    y,x,c,z=net.y,net.x,net.c,net.z
-    others=[net.xn,net.yn]
-    if column:
-        for dc in range(2):
-            for dz in range(4):
-                if dc or dz: others.append((y,x,lax.rem(c+dc,2),lax.rem(z+dz,4)))
-    else:
-        others+= [net.cn,net.zpn,net.zmn]
-    for o in others: pl.semaphore_signal(bar,inc=1,device_id=o,device_id_type=MESH)
-    pl.semaphore_wait(bar,len(others))
-
-ROWS=144; COLS=1152; TOP=80
-
-def gather_kernel(tensors, s_ref, tok_ref, cot_ref, g0, g1, g2, tok_out, cot_out, send, recv, tsend, trecv, lsem):
-    g_refs=(g0,g1,g2)
-    net=Net(); y,x,c,z=net.y,net.x,net.c,net.z
-    enter(net, True)
-    def token_copies(start):
-        for a,(src,dst) in enumerate(((tok_ref,tok_out),(cot_ref,cot_out))):
-            for i in range(2):
-                dc=lax.div(z,2); dz=2*c+i
-                here=jnp.logical_and(dc==c,dz==z)
-                rows=pl.ds(pl.multiple_of(lax.rem(z,2)*256,256),256)
-                cp=pltpu.make_async_remote_copy(src_ref=src.at[i],dst_ref=dst.at[rows],send_sem=tsend.at[a,i],recv_sem=trecv.at[a,lax.rem(z,2)],device_id=(y,x,dc,dz),device_id_type=MESH)
-                lc=pltpu.make_async_copy(src.at[i],dst.at[rows],trecv.at[a,lax.rem(z,2)])
-                @pl.when(jnp.logical_not(here))
-                def _():
-                    if start: cp.start()
-                    else: cp.wait_send()
-                @pl.when(here)
-                def _():
-                    if start: lc.start()
-    def token_arrivals():
-        for a,(src,dst) in enumerate(((tok_ref,tok_out),(cot_ref,cot_out))):
-            for k in range(2):
-                rows=pl.ds(k*256,256)
-                pltpu.make_async_copy(src.at[0],dst.at[rows],trecv.at[a,k]).wait()
-    def slot(t,yy,xx,cc,zz,part=None):
-        row=(4*yy+2*xx+cc)*ROWS
-        n=ROWS
-        if part==0: n=TOP
-        if part==1: row=row+TOP; n=ROWS-TOP
-        return g_refs[t].at[pl.ds(pl.multiple_of(row,16),n),pl.ds(pl.multiple_of(zz*COLS,COLS),COLS)]
-    counter=[0]
-    started=[]
-    def sem_of(t,yy,xx,cc,zz,part):
-        return recv.at[t,4*yy+2*xx+cc,zz,part or 0]
-    def put(dev,t,yy,xx,cc,zz,part=None,own=False):
-        src=s_ref.at[t] if own else slot(t,yy,xx,cc,zz,part)
-        cp=pltpu.make_async_remote_copy(src_ref=src,dst_ref=slot(t,yy,xx,cc,zz,part),send_sem=send.at[counter[0]],recv_sem=sem_of(t,yy,xx,cc,zz,part),device_id=dev,device_id_type=MESH)
-        counter[0]+=1
-        cp.start(); started.append(cp)
-    def arrived(t,yy,xx,cc,zz,part=None):
-        s=slot(t,yy,xx,cc,zz,part)
-        pltpu.make_async_copy(s,s,sem_of(t,yy,xx,cc,zz,part)).wait()
-    def finish():
-        for cp in started: cp.wait_send()
-        started.clear(); counter[0]=0
-    def from_partner(cc):
-        for t in range(tensors):
-            for k in range(4):
-                zz=lax.rem(z+k,4)
-                for yy in range(2):
-                    for xx in range(2):
-                        arrived(t,yy,xx,cc,zz)
-    local=[pltpu.make_async_copy(s_ref.at[t],slot(t,y,x,c,z),lsem.at[t]) for t in range(tensors)]
-    for cp in local: cp.start()
-    token_copies(True)
-    first=(y,1-x); second=(1-y,x)
-    def flow(cc):
-        near=net.xn if cc==0 else net.yn
-        far=net.yn if cc==0 else net.xn
-        nearp=(y,1-x) if cc==0 else (1-y,x)
-        farp=(1-y,x) if cc==0 else (y,1-x)
-        def when(cond,fn):
-            pl.when(cond)(fn)
-        up=z<3; down=z>0
-        def zput(dev,cond,t,zz,own=False):
-            src=s_ref.at[t] if own else slot(t,y,x,cc,zz)
-            cp=pltpu.make_async_remote_copy(src_ref=src,dst_ref=slot(t,y,x,cc,zz),send_sem=send.at[counter[0]],recv_sem=sem_of(t,y,x,cc,zz,None),device_id=dev,device_id_type=MESH)
-            counter[0]+=1
-            pl.when(cond)(cp.start); guarded.append((cond,cp))
-        guarded=[]
-        zpn=(y,x,cc,lax.rem(z+1,4)); zmn=(y,x,cc,lax.rem(z+3,4))
-        for t in range(tensors):
-            put(near,t,y,x,cc,z,own=True); put(far,t,y,x,cc,z,own=True)
-            zput(zpn,up,t,z,own=True); zput(zmn,down,t,z,own=True)
-            put(net.cn,t,y,x,cc,z,own=True)
-        def spread(t,zz):
-            put(near,t,y,x,cc,zz); put(far,t,y,x,cc,zz); put(net.cn,t,y,x,cc,zz)
-        def onward(t,zz):
-            arrived(t,nearp[0],nearp[1],cc,zz); put(far,t,nearp[0],nearp[1],cc,zz); put(net.cn,t,nearp[0],nearp[1],cc,zz)
-            arrived(t,farp[0],farp[1],cc,zz); put(net.cn,t,farp[0],farp[1],cc,zz)
-        def nth(k):
-            if k==0: return z
-            table=((1,2,3),(0,2,3),(3,1,0),(2,1,0))
-            return sum(jnp.where(z==i,table[i][k-1],0) for i in range(4))
-        for k in range(1,4):
-            zz=nth(k)
-            for t in range(tensors):
-                arrived(t,y,x,cc,zz)
-                zput(zpn,jnp.logical_and(zz<z,up),t,zz)
-                zput(zmn,jnp.logical_and(zz>z,down),t,zz)
-                spread(t,zz)
-            for t in range(tensors): onward(t,nth(k-1))
-        for t in range(tensors): onward(t,nth(3))
-        for k in range(4):
-            for t in range(tensors):
-                arrived(t,1-y,1-x,cc,nth(k)); put(net.cn,t,1-y,1-x,cc,nth(k))
-        from_partner(1-cc)
-        for cond,cp in guarded: pl.when(cond)(cp.wait_send)
-        finish()
-    @pl.when(c==0)
-    def _(): flow(0)
-    @pl.when(c==1)
-    def _(): flow(1)
-    for cp in local: cp.wait()
-    token_arrivals()
-    token_copies(False)
-
-def gather(s,tok,cot):
-    T=s.shape[0]
-    hbm=pl.BlockSpec(memory_space=pl.ANY)
-    return pl.pallas_call(functools.partial(gather_kernel,T),
-      out_shape=(jax.ShapeDtypeStruct((8*ROWS,4*COLS),jnp.bfloat16),)*3+(jax.ShapeDtypeStruct((512,COLS),tok.dtype),jax.ShapeDtypeStruct((512,COLS),cot.dtype)),
-      in_specs=[hbm]*3,out_specs=(hbm,)*5,
-      scratch_shapes=[pltpu.SemaphoreType.DMA((40*T,)),pltpu.SemaphoreType.DMA((T,8,4,2)),pltpu.SemaphoreType.DMA((2,2)),pltpu.SemaphoreType.DMA((2,2)),pltpu.SemaphoreType.DMA((T,))],
-      compiler_params=pltpu.CompilerParams(collective_id=1,has_side_effects=True))(s,tok,cot)
 HEAD_DIM=72; HS=288; KV0=256; KVW=640; AT0=768; ATW=384
 C=HEAD_DIM**-0.5; LOG2E=1.4426950408889634
 TOK=512
@@ -610,6 +469,29 @@
          M((4,TOK,HEAD_DIM),bf),M((4,2*TOK,HEAD_DIM),f32),M((4,2*TOK,HEAD_DIM),f32),M((4,TOK,KVW),bf),M((4,TOK,KVW),bf),M((TOK,COLS),bf),M((COLS,TOK),bf),M((COLS,TOK),bf),M((2,COLS,COLS),bf),
          D((2,)),D((4,)),D((4,)),D((2,))],
       compiler_params=pltpu.CompilerParams(collective_id=4,has_side_effects=True,vmem_limit_bytes=58*2**20))(x,gb,g0,qkv,kvo,att,lse)
+class OldNet:
+    def __init__(self):
+        self.y,self.x,self.c,self.z=(lax.axis_index(a) for a in AXES)
+        y,x,c,z=self.y,self.x,self.c,self.z
+        self.zp=lax.rem(z+1,4); self.zm=lax.rem(z+3,4); self.zo=lax.rem(z+2,4)
+        self.xn=(y,1-x,c,z); self.yn=(1-y,x,c,z); self.cn=(y,x,1-c,z)
+        self.zpn=(y,x,c,self.zp); self.zmn=(y,x,c,self.zm)
+
+def enter(net, column):
+    bar=pltpu.get_barrier_semaphore()
+    y,x,c,z=net.y,net.x,net.c,net.z
+    others=[net.xn,net.yn]
+    if column:
+        for dc in range(2):
+            for dz in range(4):
+                if dc or dz: others.append((y,x,lax.rem(c+dc,2),lax.rem(z+dz,4)))
+    else:
+        others+= [net.cn,net.zpn,net.zmn]
+    for o in others: pl.semaphore_signal(bar,inc=1,device_id=o,device_id_type=MESH)
+    pl.semaphore_wait(bar,len(others))
+
+ROWS=144; COLS=1152; TOP=80
+
 
 class Scatter:
     def __init__(self, net, tensors, cc, d, rc, acc, tmp, far_in, near_in, line_in, out, send, core_sem, load_sem, tmp_sem, far_sem, near_sem, line_sem):
@@ -739,7 +621,7 @@
     return each,arrivals
 
 def scatter_kernel(T, d0, d1, d2, r0, r1, out, rc, b0, b1, acc, tmp, far_in, near_in, line_in, row_send, row_recv, *sems):
-    net=Net(); enter(net,True)
+    net=OldNet(); enter(net,True)
     each,arrivals=row_copies(net,((r0,b0),(r1,b1)),row_send,row_recv)
     each(True)
     def flow(cc):
@@ -771,6 +653,514 @@
          D((2,2)),D((2,2)),D((T*36,)),D((T,2,2,4)),D((T,2,2,4)),D((2,)),D((T,2,4)),D((T,4)),D((T,2,4))],
       compiler_params=pltpu.CompilerParams(collective_id=2,has_side_effects=True,vmem_limit_bytes=58*2**20))(d0,d1,d2,r0,r1)
     return out[0],out[2],out[3]
+HEAD_DIM=72
+epsilon=1e-06
+MESH = pl.DeviceIdType.MESH
+AXES = ("y", "x", "core", "z")
+ROWS, COLS, TOK = 144, 1152, 512
+HS, KV0, KVW, AT0, ATW, ADA = 288, 256, 640, 768, 384, 1728
+C = HEAD_DIM**-0.5
+LOG2E = 1.4426950408889634
+bf = jnp.bfloat16
+f32 = jnp.float32
+VM = pl.BlockSpec(memory_space=pltpu.VMEM)
+HB = pl.BlockSpec(memory_space=pl.ANY)
+S = jax.ShapeDtypeStruct
+D = pltpu.SemaphoreType.DMA
+V = pltpu.VMEM
+
+
+def dg(a, b, ca, cb):
+    return lax.dot_general(a, b, (((ca,), (cb,)), ((), ())), preferred_element_type=f32)
+
+
+class Net:
+    def __init__(self):
+        self.y, self.x, self.c, self.z = (lax.axis_index(a) for a in AXES)
+        y, x, c, z = self.y, self.x, self.c, self.z
+        self.up, self.down = lax.rem(z + 1, 4), lax.rem(z + 3, 4)
+        self.xn, self.yn, self.dn = (y, 1 - x, c, z), (1 - y, x, c, z), (1 - y, 1 - x, c, z)
+        self.cn = (y, x, 1 - c, z)
+        self.zpn, self.zmn = (y, x, c, self.up), (y, x, c, self.down)
+        self.f, self.n = self.place(y, x)
+        self.far = self.device(1 - self.f, self.n)
+        self.near = self.device(self.f, 1 - self.n)
+
+    def place(self, a, b):
+        return (1 - self.c) * a + self.c * b, (1 - self.c) * b + self.c * a
+
+    def device(self, f, n):
+        y, x = self.place(f, n)
+        return (y, x, self.c, self.z)
+
+    def along_z(self, step):
+        return (self.y, self.x, self.c, lax.rem(self.z + step, 4))
+
+    def greet(self):
+        bar = pltpu.get_barrier_semaphore()
+        others = [self.xn, self.yn, self.dn]
+        for dc in range(2):
+            for dz in range(4):
+                if dc or dz:
+                    others.append((self.y, self.x, lax.rem(self.c + dc, 2), lax.rem(self.z + dz, 4)))
+        for o in others:
+            pl.semaphore_signal(bar, inc=1, device_id=o, device_id_type=MESH)
+        pl.semaphore_wait(bar, len(others))
+
+
+def remote(src, dst, send, recv, device):
+    return pltpu.make_async_remote_copy(
+        src_ref=src, dst_ref=dst, send_sem=send, recv_sem=recv, device_id=device, device_id_type=MESH
+    )
+
+
+def landed(ref, sem):
+    pltpu.make_async_copy(ref, ref, sem).wait()
+
+
+def gelu_pair(u):
+    k = 0.7978845608028654
+    u2 = u * u
+    t = jnp.tanh(k * u * (1.0 + 0.044715 * u2))
+    h = 0.5 * (1.0 + t)
+    return u * h, h + 0.5 * u * (1.0 - t * t) * (k * (1.0 + 3.0 * 0.044715 * u2))
+
+
+class Gather:
+    def __init__(self, net, g, shard, send, zsend, recv):
+        self.net, self.g, self.shard, self.send, self.zsend, self.recv = net, g, shard, send, zsend, recv
+
+    def slot(self, t, f, n, c, z):
+        y, x = self.net.place(f, n)
+        row = pl.multiple_of((4 * y + 2 * x + c) * ROWS, 16)
+        return self.g.at[t, pl.ds(row, ROWS), pl.ds(pl.multiple_of(z * COLS, 128), COLS)]
+
+    def sem(self, t, f, n, c, z):
+        y, x = self.net.place(f, n)
+        return self.recv.at[t, 4 * y + 2 * x + c, z]
+
+    def put(self, u, k, device, f, n, z, own=False):
+        t = lax.div(u, 4)
+        s = self.slot(t, f, n, self.net.c, z)
+        return remote(self.shard.at[t] if own else s, s, self.send.at[u, k], self.sem(t, f, n, self.net.c, z), device)
+
+    def arrived(self, t, f, n, c, z):
+        landed(self.slot(t, f, n, c, z), self.sem(t, f, n, c, z))
+
+    def nth(self, k):
+        z = self.net.z
+        after = ((0, 1, 2, 3), (1, 0, 2, 3), (2, 3, 1, 0), (3, 2, 1, 0))
+        return sum(
+            jnp.where(jnp.logical_and(z == i, k == j), after[i][j], 0)
+            for i in range(4) for j in range(4)
+        )
+
+    def onward(self, t, k, zz, act, own=False):
+        net = self.net
+        s = self.slot(t, net.f, net.n, net.c, zz)
+        src = self.shard.at[t] if own else s
+        sem = self.sem(t, net.f, net.n, net.c, zz)
+        up = jnp.logical_and(zz <= net.z, net.z < 3)
+        down = jnp.logical_and(zz >= net.z, net.z > 0)
+
+        @pl.when(up)
+        def _():
+            act(remote(src, s, self.zsend.at[t, k, 0], sem, net.zpn))
+
+        @pl.when(down)
+        def _():
+            act(remote(src, s, self.zsend.at[t, k, 1], sem, net.zmn))
+
+    def copies(self, u, own=False):
+        net = self.net
+        zz = net.z if own else self.nth(lax.rem(u, 4))
+        f, n = net.f, net.n
+        return (
+            [self.put(u, 0, net.near, f, n, zz, own), self.put(u, 1, net.far, f, n, zz, own), self.put(u, 2, net.cn, f, n, zz, own)],
+            [self.put(u, 3, net.far, f, 1 - n, zz), self.put(u, 4, net.cn, f, 1 - n, zz), self.put(u, 5, net.cn, 1 - f, n, zz)],
+            [self.put(u, 6, net.cn, 1 - f, 1 - n, zz)],
+        )
+
+    def line(self, u):
+        t, k = lax.div(u, 4), lax.rem(u, 4)
+        pl.when(k == 0)(lambda: self.onward(t, k, self.net.z, lambda cp: cp.start(), True))
+
+        @pl.when(k > 0)
+        def _():
+            zz = self.nth(k)
+            self.arrived(t, self.net.f, self.net.n, self.net.c, zz)
+            self.onward(t, k, zz, lambda cp: cp.start())
+
+    def spread(self, u):
+        k = lax.rem(u, 4)
+
+        @pl.when(k == 0)
+        def _():
+            for cp in self.copies(u, True)[0]:
+                cp.start()
+
+        @pl.when(k > 0)
+        def _():
+            for cp in self.copies(u)[0]:
+                cp.start()
+
+    def across(self, u):
+        net, t = self.net, lax.div(u, 4)
+        zz = self.nth(lax.rem(u, 4))
+        a, b, d = self.copies(u)[1]
+        self.arrived(t, net.f, 1 - net.n, net.c, zz)
+        a.start()
+        b.start()
+        self.arrived(t, 1 - net.f, net.n, net.c, zz)
+        d.start()
+
+    def corner(self, u):
+        net, t = self.net, lax.div(u, 4)
+        self.arrived(t, 1 - net.f, 1 - net.n, net.c, self.nth(lax.rem(u, 4)))
+        self.copies(u)[2][0].start()
+
+    def do(self, *steps):
+        for name, u in steps:
+            getattr(self, name)(jnp.int32(u))
+
+    def at(self, point, table):
+        for p, steps in enumerate(table):
+            pl.when(point == p)(lambda: self.do(*steps))
+
+    def from_mate(self, t):
+        def one(i, _):
+            self.arrived(t, lax.div(i, 8), lax.rem(lax.div(i, 4), 2), 1 - self.net.c, lax.rem(i, 4))
+            return 0
+
+        lax.fori_loop(0, 16, one, 0)
+
+    def finish(self):
+        def one(u, _):
+            for group in self.copies(u):
+                for cp in group:
+                    cp.wait_send()
+            t, k = lax.div(u, 4), lax.rem(u, 4)
+            self.onward(t, k, self.nth(k), lambda cp: cp.wait_send())
+            return 0
+
+        lax.fori_loop(0, 12, one, 0)
+
+
+def rows_out(net, i):
+    dc, dz = lax.div(net.z, 2), 2 * net.c + i
+    here = jnp.logical_and(dc == net.c, dz == net.z)
+    return (net.y, net.x, dc, dz), pl.multiple_of(lax.rem(net.z, 2) * 256, 256), here
+
+
+class Rows:
+    def __init__(self, net, src, dst, send, recv):
+        self.net, self.src, self.dst, self.send, self.recv = net, src, dst, send, recv
+
+    def each(self, start):
+        for i in range(2):
+            device, row, here = rows_out(self.net, i)
+            rows = self.dst.at[pl.ds(row, 256)]
+            sem = self.recv.at[lax.rem(self.net.z, 2)]
+
+            @pl.when(jnp.logical_not(here))
+            def _():
+                cp = remote(self.src.at[i], rows, self.send.at[i], sem, device)
+                cp.start() if start else cp.wait_send()
+
+            if start:
+
+                @pl.when(here)
+                def _():
+                    rows[...] = self.src[i]
+
+    def arrivals(self):
+        net = self.net
+        for k in range(2):
+            here = jnp.logical_and(lax.div(net.z, 2) == net.c, 2 * net.c + k == net.z)
+            pl.when(jnp.logical_not(here))(lambda: landed(self.dst.at[pl.ds(k * 256, 256)], self.recv.at[k]))
+
+
+def normalize(v):
+    mean = jnp.mean(v, axis=-1, keepdims=True)
+    centred = v - mean
+    r = lax.rsqrt(jnp.mean(centred * centred, axis=-1, keepdims=True) + epsilon)
+    return centred * r, r
+
+
+def by_rows(step, body):
+    def one(i, _):
+        body(pl.ds(pl.multiple_of(i * step, step), step))
+        return 0
+
+    lax.fori_loop(0, TOK // step, one, 0)
+
+
+TABLE = (
+    (("line", 7), ("line", 8), ("spread", 7), ("spread", 8), ("across", 6)),
+    (("corner", 5),),
+    (("line", 9), ("corner", 6)),
+    (("across", 7), ("line", 10), ("spread", 9)),
+    (("line", 11), ("across", 8), ("corner", 7)),
+    (("spread", 10),),
+    (("spread", 11), ("corner", 8)),
+    (("across", 9),),
+    (("across", 10), ("corner", 9)),
+    (("across", 11), ("corner", 10)),
+    (("corner", 11),),
+)
+
+
+def forward_kernel(
+    shard, tokens, cotangent, lift_own, ada, ada_bias, z_bias, out_bias,
+    g, tok, cot, lift_rows, vectors, biases, x_out, qkv_out, kvo_out, att_out, lse, peak, branch_out, nm_out, act_out, gd_out, d2,
+    tok_v, cot_v, lift, part, part_in, four, four_in, zall, x_ref, w, qkv, kvo, att, branch, qh, kh, vh, oh, gbt, act_buf, gd_buf, dbuf,
+    gsend, gzsend, grecv, lsem, rsend, rrecv, small_send, small_recv, wsem, ksend, krecv, osem, asem, gdsem, dsem,
+):
+    net = Net()
+    y, x, c, z = net.y, net.x, net.c, net.z
+    plane = 2 * y + x
+    net.greet()
+    flow = Gather(net, g, shard, gsend, gzsend, grecv)
+    lift[plane, c] = lift_own[...]
+    small = [remote(lift.at[plane, c], lift.at[plane, c], small_send.at[0], small_recv.at[0], net.cn)]
+    small[0].start()
+    token_rows = Rows(net, tokens, tok_v, rsend.at[0], rrecv.at[0])
+    cot_rows = Rows(net, cotangent, cot_v, rsend.at[1], rrecv.at[1])
+    flow.do(("line", 0))
+    own = [pltpu.make_async_copy(shard.at[t], flow.slot(t, net.f, net.n, c, z), lsem.at[t]) for t in range(3)]
+    for cp in own:
+        cp.start()
+
+    landed(lift.at[plane, 1 - c], small_recv.at[0])
+    peers = ((net.xn, 2 * y + 1 - x), (net.yn, 2 - 2 * y + x), (net.dn, 3 - plane))
+    for k, (dev, _) in enumerate(peers):
+        cp = remote(lift.at[plane], lift.at[plane], small_send.at[1 + k], small_recv.at[1 + k], dev)
+        cp.start()
+        small.append(cp)
+    flow.do(("spread", 0), ("spread", 4), ("line", 1))
+    for k, (_, p) in enumerate(peers):
+        landed(lift.at[p], small_recv.at[1 + k])
+    every = jnp.concatenate([lift[p, k, 0:2] for p in range(4) for k in range(2)], axis=0).astype(bf)
+    batch = 4 * y + 2 * x + c
+    pick = lax.broadcasted_iota(jnp.int32, (COLS, ROWS), 0) == lax.broadcasted_iota(jnp.int32, (COLS, ROWS), 1) + batch * ROWS
+    rows = dg(every, jnp.where(pick, 1.0, 0.0).astype(bf), 1, 0)
+    lift_rows[...] = rows
+    partial = dg(rows.astype(bf), ada[...], 1, 0)
+    part[...] = jnp.zeros_like(part)
+    for p in range(4):
+        part[p, 0:4] = partial[4 * p : 4 * p + 4]
+    for k, (dev, p) in enumerate(peers):
+        cp = remote(part.at[p], part_in.at[k], small_send.at[4 + k], small_recv.at[4 + k], dev)
+        cp.start()
+        small.append(cp)
+    flow.do(("spread", 1), ("line", 2), ("across", 0))
+    token_rows.each(True)
+    flow.do(("spread", 2), ("line", 3))
+    for k in range(3):
+        landed(part_in.at[k], small_recv.at[4 + k])
+    four[...] = part[plane] + part_in[0] + part_in[1] + part_in[2]
+    cp = remote(four, four_in, small_send.at[7], small_recv.at[7], net.cn)
+    cp.start()
+    small.append(cp)
+    flow.do(("across", 4), ("line", 4), ("spread", 3), ("across", 1), ("corner", 0))
+    landed(four_in, small_recv.at[7])
+    zall[z] = four[...] + four_in[...] + ada_bias[...]
+    zall[z, 4:5] = z_bias[...]
+    for k in range(3):
+        cp = remote(zall.at[z], zall.at[z], small_send.at[8 + k], small_recv.at[8 + k], net.along_z(k + 1))
+        cp.start()
+        small.append(cp)
+    flow.do(("across", 2), ("corner", 4))
+    for k in range(3):
+        landed(zall.at[lax.rem(z + 3 - k, 4)], small_recv.at[8 + k])
+    pieces = [zall[k, pl.ds(z, 1)] for k in range(4)]
+    half = COLS // 2
+    vectors[0:1] = pieces[0][:, :COLS]
+    vectors[1:2] = jnp.concatenate([pieces[0][:, COLS:], pieces[1][:, :half]], axis=1)
+    vectors[2:3] = pieces[1][:, half:]
+    vectors[3:4] = pieces[2][:, :COLS]
+    vectors[4:5] = jnp.concatenate([pieces[2][:, COLS:], pieces[3][:, :half]], axis=1)
+    vectors[5:6] = pieces[3][:, half:]
+    vectors[6:8] = jnp.zeros((2, COLS), f32)
+    nothing = jnp.zeros((1, HS), f32)
+    for k in range(4):
+        b = zall[k, 4:5]
+        biases[k, 0:1] = jnp.concatenate([b[:, :HS], nothing, b[:, HS : 2 * HS], nothing], axis=1)
+        biases[k, 1:2] = b[:, 2 * HS :]
+
+    flow.do(("across", 3), ("corner", 1), ("line", 5), ("spread", 5), ("corner", 2))
+    token_rows.arrivals()
+
+    def first_norm(r):
+        n, _ = normalize(tok_v[r].astype(f32))
+        x_ref[r] = (n * (1.0 + vectors[1:2]) + vectors[0:1]).astype(bf)
+
+    by_rows(64, first_norm)
+    outs = [pltpu.make_async_copy(x_ref, x_out, osem.at[1]), pltpu.make_async_copy(tok_v, tok, osem.at[0])]
+    for cp in outs:
+        cp.start()
+    flow.do(("corner", 3), ("line", 6), ("spread", 6), ("across", 5))
+    flow.from_mate(0)
+
+    def load_w(t, k):
+        return pltpu.make_async_copy(g.at[t, :, pl.ds(k * COLS, COLS)], w.at[k], wsem.at[k])
+
+    own[0].wait()
+    for k in range(4):
+        load_w(0, k).start()
+
+    def kv(k):
+        return remote(qkv.at[k, :, pl.ds(KV0, KVW)], kvo.at[k], ksend.at[k], krecv.at[k], net.cn)
+
+    for k in range(4):
+        load_w(0, k).wait()
+        qkv[k] = (dg(x_ref[...], w[k], 1, 0) + biases[k, 0:1]).astype(bf)
+        kv(k).start()
+    cp = pltpu.make_async_copy(qkv, qkv_out, osem.at[2])
+    cp.start()
+    outs.append(cp)
+    branch[...] = jnp.broadcast_to(out_bias[...], (TOK, COLS))
+
+
+    def chunk(k, _):
+        flow.at(2 * k, TABLE)
+        pl.when(k == 2)(lambda: cot_rows.each(True))
+        kv(k).wait_recv()
+        for j in range(4):
+            a = j * HEAD_DIM
+            qh[j] = qkv[k, :, a : a + HEAD_DIM]
+            kh[j, :TOK] = qkv[k, :, HS + a : HS + a + HEAD_DIM]
+            vh[j, :TOK] = qkv[k, :, 2 * HS + a : 2 * HS + a + HEAD_DIM]
+            kh[j, TOK:] = kvo[k, :, HS - KV0 + a : HS - KV0 + a + HEAD_DIM]
+            vh[j, TOK:] = kvo[k, :, 2 * HS - KV0 + a : 2 * HS - KV0 + a + HEAD_DIM]
+
+        def head(j, _):
+            h = k * 4 + j
+            s = dg(kh[j], qh[j], 1, 1)
+            m = jnp.max(s, axis=0, keepdims=True)
+            p = jnp.exp2((s - m) * (C * LOG2E))
+            l = jnp.sum(p, axis=0, keepdims=True)
+            o = dg(vh[j], p.astype(bf), 0, 0) / l
+            oh[j] = o.T.astype(bf)
+            lse[h] = m * (C * LOG2E) + jnp.log2(l)
+            peak[h] = jnp.broadcast_to(jnp.max(m, axis=1, keepdims=True) * C, (1, 128))
+            pl.when(j == 1)(lambda: flow.at(2 * k + 1, TABLE))
+            return 0
+
+        lax.fori_loop(0, 4, head, 0)
+        att[k] = jnp.concatenate([jnp.zeros((TOK, ATW - HS), bf)] + [oh[j] for j in range(4)], axis=1)
+        branch[...] += dg(att[k], w[k, :, AT0:], 1, 1)
+        return 0
+
+    lax.fori_loop(0, 4, chunk, 0)
+    for src, dst, k in ((kvo, kvo_out, 3), (att, att_out, 4), (branch, branch_out, 5)):
+        cp = pltpu.make_async_copy(src, dst, osem.at[k])
+        cp.start()
+        outs.append(cp)
+    outs[0].wait()
+
+    def second_norm(r):
+        after = tok_v[r].astype(f32) + vectors[2:3] * branch[r]
+        n, _ = normalize(after)
+        x_ref[r] = (n * (1.0 + vectors[4:5]) + vectors[3:4]).astype(bf)
+
+    by_rows(64, second_norm)
+    cp = pltpu.make_async_copy(x_ref, nm_out, osem.at[6])
+    cp.start()
+    outs[0] = cp
+    flow.from_mate(1)
+    own[1].wait()
+    for k in range(4):
+        load_w(1, k).start()
+
+    def slope_store(k):
+        i = lax.rem(k, 2)
+        return pltpu.make_async_copy(gd_buf.at[i], gd_out.at[k], gdsem.at[i])
+
+    def hidden(k, _):
+        i = lax.rem(k, 2)
+        pltpu.make_async_copy(g.at[1, :, pl.ds(pl.multiple_of(k * COLS, 128), COLS)], w.at[k], wsem.at[k]).wait()
+        pl.when(k >= 2)(lambda: slope_store(k - 2).wait())
+        gd_buf[i] = dg(x_ref[...], w[k], 1, 0)
+
+        def activate(r):
+            a, d = gelu_pair(gd_buf[i, r] + biases[k, 1:2])
+            act_buf[k, r] = a.astype(bf)
+            gd_buf[i, r] = d
+
+        by_rows(64, activate)
+        slope_store(k).start()
+        pltpu.make_async_copy(act_buf.at[k], act_out.at[k], asem.at[k]).start()
+        flow.at(8 + k, TABLE)
+        return 0
+
+    lax.fori_loop(0, 4, hidden, 0)
+    cot_rows.arrivals()
+    cp = pltpu.make_async_copy(cot_v, cot, osem.at[1])
+    cp.start()
+    outs.append(cp)
+
+    def gated(r):
+        x_ref[r] = (vectors[5:6] * cot_v[r].astype(f32)).astype(bf)
+
+    outs[0].wait()
+    by_rows(64, gated)
+    gbt[...] = x_ref[...].T
+
+    def down_store(k):
+        i = lax.rem(k, 2)
+        return pltpu.make_async_copy(dbuf.at[i], d2.at[:, pl.ds(pl.multiple_of(k * COLS, 128), COLS)], dsem.at[i])
+
+    def down(k, _):
+        i = lax.rem(k, 2)
+        pl.when(k >= 2)(lambda: down_store(k - 2).wait())
+        dbuf[i] = dg(gbt[...], act_buf[k], 1, 0).astype(bf)
+        down_store(k).start()
+        return 0
+
+    lax.fori_loop(0, 4, down, 0)
+    for k in (2, 3):
+        slope_store(k).wait()
+        down_store(k).wait()
+    for k in range(4):
+        pltpu.make_async_copy(act_buf.at[k], act_out.at[k], asem.at[k]).wait()
+    flow.from_mate(2)
+    flow.finish()
+    for cp in outs[1:]:
+        cp.wait()
+    for k in range(4):
+        kv(k).wait_send()
+    for cp in small:
+        cp.wait_send()
+    own[2].wait()
+    token_rows.each(False)
+    cot_rows.each(False)
+
+
+def forward(shard, tokens, cotangent, lift_own, ada, ada_bias, z_bias, out_bias):
+    rows = S((TOK, COLS), bf)
+    wide = S((TOK, COLS), f32)
+    return pl.pallas_call(
+        forward_kernel,
+        name="forward",
+        out_shape=(
+            S((3, 8 * ROWS, 4 * COLS), bf), rows, rows, S((16, ROWS), f32), S((8, COLS), f32), S((4, 2, COLS), f32),
+            rows, S((4, TOK, COLS), bf), S((4, TOK, KVW), bf), S((4, TOK, ATW), bf), S((16, 1, TOK), f32),
+            S((16, 1, 128), f32), wide, rows, S((4, TOK, COLS), bf), S((4, TOK, COLS), f32), S((8 * ROWS, 4 * COLS), bf),
+        ),
+        in_specs=[VM] * 8,
+        out_specs=(HB, HB, HB, VM, VM, VM, HB, HB, HB, HB, VM, VM, HB, HB, HB, HB, HB),
+        scratch_shapes=[
+            V((TOK, COLS), bf), V((TOK, COLS), bf), V((4, 2, 8, COLS), f32), V((4, 8, ADA), f32), V((3, 8, ADA), f32),
+            V((8, ADA), f32), V((8, ADA), f32), V((4, 8, ADA), f32), V((TOK, COLS), bf), V((4, COLS, COLS), bf),
+            V((4, TOK, COLS), bf), V((4, TOK, KVW), bf), V((4, TOK, ATW), bf), V((TOK, COLS), f32),
+            V((4, TOK, HEAD_DIM), bf), V((4, 2 * TOK, HEAD_DIM), bf), V((4, 2 * TOK, HEAD_DIM), bf), V((4, TOK, HEAD_DIM), bf),
+            V((COLS, TOK), bf), V((4, TOK, COLS), bf), V((2, TOK, COLS), f32), V((2, COLS, COLS), bf),
+            D((12, 7)), D((3, 4, 2)), D((3, 8, 4)), D((3,)), D((2, 2)), D((2, 2)), D((11,)), D((11,)), D((4,)), D((4,)), D((4,)),
+            D((7,)), D((4,)), D((2,)), D((2,)),
+        ],
+        compiler_params=pltpu.CompilerParams(collective_id=1, has_side_effects=True, vmem_limit_bytes=60 * 2**20),
+    )(shard, tokens, cotangent, lift_own, ada, ada_bias, z_bias, out_bias)
 
 def modulate(values, shift, scale):
     average = jnp.mean(values, axis=-1, keepdims=True)
@@ -788,31 +1178,19 @@
     batch = 4 * y + 2 * x + c
     first = jnp.concatenate([query_weight, key_weight, value_weight, out_weight.T], axis=1)
     shard = jnp.stack([first, up_weight, down_weight.T])
-    full0, full1, full2, own_tokens, own_cotangent = gather(shard, tokens, cotangent)
-
-    lifted = jax.nn.silu(conditioning).astype(bf)
-    every_lifted = lax.all_gather(lifted, ("y", "x", "core"), axis=0, tiled=True)
-    lifted_rows = lax.dynamic_slice(every_lifted, (0, batch * ROWS), (16, ROWS))
-    partial = product(lifted_rows, ada_weight)
-    columns = lax.psum(partial, ("y", "x", "core")) + ada_bias
-    four = lax.dynamic_slice(columns, (4 * plane, 0), (4, columns.shape[1]))
-    biases = jnp.concatenate([query_bias, value_bias, up_bias])[None]
-    by_z = lax.all_gather(jnp.concatenate([four, biases]), "z", axis=0)
-    vectors = lax.dynamic_slice(by_z, (0, z, 0), (4, 1, by_z.shape[2])).reshape(6, 1, COLS)
-    shift_attn, scale_attn, gate_attn, shift_mlp, scale_mlp, gate_mlp = vectors
-    all_bias = by_z[:, 4]
-    nothing = jnp.zeros((4, HS), f32)
-    bias0 = jnp.concatenate([all_bias[:, :HS], nothing, all_bias[:, HS : 2 * HS], nothing], axis=1)
-    full_up_bias = all_bias[:, 2 * HS :].reshape(1, 4 * COLS)
-
+    lift_own = jnp.pad(jax.nn.silu(conditioning).astype(bf).astype(f32), ((0, 6), (0, 0)))
+    z_bias = jnp.concatenate([query_bias, value_bias, up_bias])[None]
+    (
+        full, own_tokens, own_cotangent, lifted_rows, vectors, biases, normed_attn, qkv, mate_kv, attended, totals,
+        peak, branch_attn, normed_mlp, active, slope, grad_down,
+    ) = forward(shard, tokens, cotangent, lift_own, ada_weight, ada_bias[None], z_bias, out_bias[None])
+    lifted_rows = lifted_rows.astype(bf)
+    shift_attn, scale_attn, gate_attn, shift_mlp, scale_mlp, gate_mlp = [vectors[i : i + 1] for i in range(6)]
+    full0, full1, full2 = full[0], full[1], full[2]
     inputs = own_tokens.astype(f32)
-    normed_attn = modulate(inputs, shift_attn, scale_attn).astype(bf)
-    qkv, mate_kv, attended, totals, peak, branch_attn = att_fwd(normed_attn, full0, bias0[:, None])
-    branch_attn = branch_attn + out_bias
     after_attn = inputs + gate_attn * branch_attn
-    normed_mlp = modulate(after_attn, shift_mlp, scale_mlp).astype(bf)
-    upward = product(normed_mlp, full1) + full_up_bias
-    active = jax.nn.gelu(upward, approximate=True).astype(bf)
+    active = jnp.swapaxes(active, 0, 1).reshape(TOK, 4 * COLS)
+    slope = jnp.swapaxes(slope, 0, 1).reshape(TOK, 4 * COLS)
     branch_mlp = against(active, full2) + down_bias
     block_out = (after_attn + gate_mlp * branch_mlp).astype(bf)
 
@@ -820,10 +1198,8 @@
     grad_branch_mlp = (gate_mlp * grad_out).astype(bf)
     grad_gate_mlp = jnp.sum(grad_out * branch_mlp, axis=0)
     grad_down_bias = jnp.sum(grad_branch_mlp, axis=0, dtype=f32)
-    grad_down = inner_rows(grad_branch_mlp, active).astype(bf)
     grad_active = product(grad_branch_mlp, full2)
-    _, gelu_pull = jax.vjp(partial_gelu, upward)
-    grad_upward = gelu_pull(grad_active)[0].astype(bf)
+    grad_upward = (grad_active * slope).astype(bf)
     grad_up_bias = jnp.sum(grad_upward, axis=0, dtype=f32)
     grad_up = inner_rows(normed_mlp, grad_upward).astype(bf)
     grad_normed_mlp = against(grad_upward, full1)

time: 769 us -> 741 us (0.964)
  local copies, waits for them, and re-layouts: 11.9 us -> 59.1 us
  matrix products: 80.3 us -> 52.1 us
  Pallas kernels: 468 us -> 444 us
  blocking collectives: 160 us -> 139 us
  between operations: 15.4 us -> 2.07 us
  other arithmetic: 23.1 us -> 30.8 us
    pallas_call x2 -> x1, Pallas kernels: 208 us -> 183 us  [forward(): pl.pallas_call(forward_kernel, name='forward', out_shape=(S((3, 8 * ROWS,...]
    all_gather x2 -> x0, blocking collectives: 23.4 us -> none  [the longest x1 14.3 us: one_image_per_chip(): by_z = lax.all_gather(jnp.concatenate([four, biases]), 'z', axis=0)]
    dot_general x3 -> x1, matrix products: 28.9 us -> 11.5 us  [product(): return jnp.dot(left, right, preferred_element_type=jnp.float32)]
    transpose x0 -> x2, local copies, waits for them, and re-layouts: none -> 16.3 us  [the longest x1 9.59 us: one_image_per_chip(): slope = jnp.swapaxes(slope, 0, 1).reshape(TOK, 4 * COLS)]
    squeeze x0 -> x1, local copies, waits for them, and re-layouts: none -> 9.82 us  [one_image_per_chip(): full0, full1, full2 = (full[0], full[1], full[2])]
    reshape x1, local copies, waits for them, and re-layouts: 0.1 us -> 9.6 us  [one_image_per_chip(): slope = jnp.swapaxes(slope, 0, 1).reshape(TOK, 4 * COLS)]
    dot_general x3 -> x2, matrix products: 21.5 us -> 12.2 us  [inner_rows(): lax.dot_general(left, right, (((0,), (0,)), ((), ())), preferred_element_...]
  transfers between devices with their start and end apart: 1 -> 0, of which waited for: 0 -> 0; matrix products, arithmetic and copies ran while one was open for 1% -> 0% of each run, Pallas kernels for 21% -> 0%
where the time goes in v2:
time: 741 us; the launch traced here: 727 us
  Pallas kernels  444 us (60%)
  blocking collectives  139 us (19%)
  local copies, waits for them, and re-layouts  59.1 us (8%)
  matrix products  52.1 us (7%)
  other arithmetic  30.8 us (4%)
    pallas_call x1, Pallas kernels, scatter(): pl.pallas_call(functools.partial(scatter_kernel, T), name='scatter', out_...  187 us
    pallas_call x1, Pallas kernels, forward(): pl.pallas_call(forward_kernel, name='forward', out_shape=(S((3, 8 * ROWS,...  183 us
    pallas_call x1, Pallas kernels, att_bwd(): pl.pallas_call(att_bwd_kernel, name='att_bwd', out_shape=(S((COLS, 4 * CO...  74.1 us
    pmax x1, blocking collectives, one_image_per_chip(): peaks = lax.pmax(peak[:, 0, 0], AXES)  46.2 us
    psum x1, blocking collectives, one_image_per_chip(): bias_total = lax.psum(bias_vector, AXES)  38.5 us
    dot_general x3, matrix products, against(): lax.dot_general(left, right, (((1,), (1,)), ((), ())), preferred_element_...  28.4 us
    psum x1, blocking collectives, one_image_per_chip(): grad_lifted = lax.psum(against(grad_modulation, ada_weight), 'z')  16.4 us

profile of v2, /device:TPU:28, one launch (start us, length us, event | category | flops | bytes accessed | tf_op | source)
XLA Modules:
  0.0 727.2 jit_solution(5899481544976155603)
XLA Ops:
  2.0 2.2 pad_maximum_fusion.shard
  6.7 183.0 %forward.1 = (bf16[3,1152,4608]{2,1,0:T(8,128)(2,1)}, bf16[512,1152]{1,0:T(8,128)(2,1)}, bf16[512,1152]{1,0:T(8,128)(2,1)}, f32[16,144]{1,0:T(8,128)}, f32[8,115...) custom-call(bf16[3,144,1152]{2,1,0:T(8,128)(2,1)} %pad_maximum_fusio, ...), custom_call_target="tpu_custom_call" | custom-call | tf_op jit(solution)/shard_map/forward/pallas_call | solution.py:1143
  189.8 1.6 add_reduce_fusion
  191.3 6.7 copy.47
  198.1 13.6 %add_convert_fusion.1 = (bf16[512,1152]{1,0:T(8,128)(2,1)}, f32[512,1152]{1,0:T(8,128)S(1)}, f32[512]{0:T(512)}, f32[512,1152]{1,0:T(8,128)}) fusion(f32[1152]{0:T(1024)} %get-tuple-element.76, f32[512,1152]{1,0:T(8,128)} %get-tuple-element.47, f32[1152]{0:T(1024)} %get-tuple-element.77, bf16[512,1152]{1,0:T(8,128)(2,1)S(1)} %copy-done.2, f32[1152]{0:T(1024)} %param.31, ...), kind=kOutput, calls=%fused_computation.37 | convolution fusion | flops 5440536064 | bytes 24799232 | tf_op jit(solution)/shard_map/dot_general | solution.py:33
  215.4 9.6 %copy.45 = f32[512,4,1152]{0,2,1:T(8,128)} copy(f32[512,4,1152]{2,0,1:T(8,128)} %bitcast.67) | data formatting | bytes 18874368 | tf_op jit(solution)/shard_map/transpose | solution.py:1193
  225.0 9.6 %copy.46 = f32[512,4608]{1,0:T(8,128)} copy(f32[512,4608]{0,1:T(8,128)} %bitcast.66) | data formatting | bytes 18874368 | tf_op jit(solution)/shard_map/reshape | solution.py:1193
  234.6 11.5 %convert_reduce_fusion = (f32[4608]{0:T(1024)}, bf16[512,4608]{1,0:T(8,128)(2,1)S(1)}) fusion(f32[512,4608]{1,0:T(8,128)} %copy.46, bf16[3,1152,4608]{2,1,0:T(8,128)(2,1)} %get-tuple-element.44, bf16[512,1152]{1,0:T(8,128)(2,1)} %get-tuple-element.43, f32[1152]{0:T(1024)} %get-tuple-element.76), kind=kOutput, calls=%fused_computation.9 | convolution fusion | flops 5447020032 | bytes 25978880 | tf_op jit(solution)/shard_map/dot_general | solution.py:23
  246.2 12.8 %multiply_reduce_fusion = (f32[1152]{0:T(1024)}, f32[512]{0:T(512)S(1)}, f32[1152]{0:T(1024)}, f32[512,1152]{1,0:T(8,128)S(1)}) fusion(f32[512,1152]{1,0:T(8,128)S(1)} %get-tuple-element.81, f32[512]{0:T(512)S(1)} %copy-done.22, f32[512]{0:T(512)S(1)} %copy-done.18, f32[1152]{0:T(1024)S(1)} %get-tuple-element.75, ...), kind=kOutput, calls=%fused_computation.34 | convolution fusion | flops 5440534016 | bytes 20073984 | tf_op jit(solution)/shard_map/dot_general | solution.py:33
  259.1 2.5 fusion.36
  262.5 2.6 convert_reduce_fusion.2
  265.2 9.8 %slice_bitcast_fusion.g0_ref = bf16[1152,4608]{1,0:T(8,128)(2,1)} fusion(bf16[3,1152,4608]{2,1,0:T(8,128)(2,1)} %get-tuple-element.44), kind=kLoop, calls=%fused_computation.7 | loop fusion | bytes 21233664 | tf_op jit(solution)/shard_map/squeeze | solution.py:1189
  275.0 74.1 %att_bwd.1 = (bf16[1152,4608]{1,0:T(8,128)(2,1)}, f32[512,1152]{1,0:T(8,128)}, f32[4,1,1152]{2,1,0:T(1,128)}) custom-call(bf16[512,1152]{1,0:T(8,128)(2,1)} %get-tuple-element.41.x_ref, bf16[512,1152]{1,0:T(8,128)(2,1)} %get-tuple-element.85.gb_ref, bf16[1152,4608]{1,0:T(8,128)(2,1)} %slice_bitcast_fusion.g0_ref, ...), custom_call_target="tpu_custom_call" | custom-call | tf_op jit(solution)/shard_map/att_bwd/pallas_call | solution.py:465
  353.2 38.5 %psum.23 = f32[11520]{0:T(1024)} all-reduce(f32[11520]{0:T(1024)} %pad_maximum_fusion.1), channel_id=1, replica_groups=mesh['y'=2,'x'=2,'core'=2,'z'=4] {'y','x','core','z'}, use_global_device_ids=true, to_apply=%region_19.20 | all-reduce | flops 11520 | bytes 92160 | tf_op jit(solution)/shard_map/psum | solution.py:1245
  391.7 1.4 fusion.37
  393.1 1.5 fusion.38
  394.6 2.4 fusion.20
  397.1 1.7 fusion.23
  403.9 1.5 reshape.122
  405.3 4.6 psum.21
  409.9 14.6 %all-gather.2 = bf16[4,4,1728]{2,1,0:T(4,128)(2,1)} all-gather(bf16[1,4,1728]{2,1,0:T(4,128)(2,1)} %bitcast.74), channel_id=2, replica_groups=mesh['y'=2,'x'=2,'core'=2,'z'=4] {'z'}, dimensions={0}, use_global_device_ids=true | all-gather | bytes 69120 | tf_op jit(solution)/shard_map/all_gather | solution.py:1230
  425.4 8.5 %all-gather.1 = bf16[16,1,1728]{2,1,0:T(2,128)(2,1)S(1)} all-gather(bf16[4,1,1728]{2,1,0:T(2,128)(2,1)S(1)} %constant_dynamic-slice_fusion), channel_id=3, replica_groups=mesh['y'=2,'x'=2,'core'=2,'z'=4] {'y','x'}, dimensions={0}, use_global_device_ids=true | all-gather | bytes 69120 | tf_op jit(solution)/shard_map/all_gather | solution.py:1232
  433.9 2.0 fusion.25
  435.9 1.9 convolution_bitcast_fusion
  437.9 16.4 %psum.22 = f32[1,16,144]{2,1,0:T(8,128)} all-reduce(f32[1,16,144]{2,1,0:T(8,128)} %convolution_bitcast_fusion), channel_id=1, replica_groups=mesh['y'=2,'x'=2,'core'=2,'z'=4] {'z'}, use_global_device_ids=true, to_apply=%region_15.16 | all-reduce | flops 2304 | bytes 18432 | tf_op jit(solution)/shard_map/psum | solution.py:1235
  454.2 10.0 %all_gather.19 = f32[8,16,144]{2,1,0:T(8,128)} all-gather(f32[1,16,144]{2,1,0:T(8,128)} %psum.22), channel_id=1, replica_groups=mesh['y'=2,'x'=2,'core'=2,'z'=4] {'y','x','core'}, dimensions={0}, use_global_device_ids=true | all-gather | bytes 82944 | tf_op jit(solution)/shard_map/all_gather | solution.py:1236
  468.4 1.5 convert_reduce_fusion.4
  470.6 3.8 add_convert_fusion.r1
  474.5 10.2 %convolution_convert_fusion.d1 = bf16[1152,4608]{1,0:T(8,128)(2,1)} fusion(bf16[512,1152]{1,0:T(8,128)(2,1)S(1)} %copy-done.33, bf16[512,4608]{1,0:T(8,128)(2,1)} %copy-done.34), kind=kOutput, calls=%fused_computation | convolution fusion | flops 5441126400 | bytes 16515072 | tf_op jit(solution)/shard_map/dot_general | solution.py:27
  484.7 187.2 %scatter.1 = (f32[3,144,1152]{2,1,0:T(8,128)}, bf16[3,2,2,4,144,1152]{5,4,3,2,1,0:T(8,128)(2,1)}, bf16[2,256,1152]{2,1,0:T(8,128)(2,1)}, bf16[2,256,1152]{2,1,0:T(8,128)(2,1)}) custom-call(bf16[1152,4608]{1,0:T(8,128)(2,1)} %get-tuple-element.52.d0, bf16[1152,4608]{1,0:T(8,128)(2,1)} %convolution_convert_fusion.d1, bf16[1152,4608]{1,0:T(8,128)(2,1)} %get-tuple-element.54.d2, ...), custom_call_target="tpu_custom_call" | custom-call | tf_op jit(solution)/shard_map/scatter/pallas_call | solution.py:649
  671.9 3.0 convert_element_type.72
  677.3 46.2 %pmax.7 = f32[16]{0:T(128)S(1)} all-reduce(f32[16]{0:T(128)S(1)} %slice_reduce_fusion), channel_id=1, replica_groups=mesh['y'=2,'x'=2,'core'=2,'z'=4] {'y','x','core','z'}, use_global_device_ids=true, to_apply=%region_21.22 | all-reduce | flops 16 | bytes 128 | tf_op jit(solution)/shard_map/pmax | solution.py:1253
  (109 shorter events, 28.4 us)
Async XLA Ops:
  0.7 3.5 copy-start.11
  0.7 4.2 copy-start.23
  0.7 4.2 copy-start.31
  0.7 4.2 copy-start.25
  0.7 4.8 copy-start.30
  0.7 5.4 copy-start.26
  191.3 6.7 copy-start.2
  211.7 34.5 %copy-start.1 = (f32[512,1152]{1,0:T(8,128)}, f32[512,1152]{1,0:T(8,128)S(1)}, u32[]{:S(2)}) copy-start(f32[512,1152]{1,0:T(8,128)S(1)} %get-tuple-element.81) | copy-start | bytes 7077892
  234.6 11.6 %copy-start.18 = (f32[512]{0:T(512)S(1)}, f32[512]{0:T(512)}, u32[]{:S(2)}) copy-start(f32[512]{0:T(512)} %copy-done.17) | copy-start | bytes 6148
  234.6 11.6 %copy-start.22 = (f32[512]{0:T(512)S(1)}, f32[512]{0:T(512)}, u32[]{:S(2)}) copy-start(f32[512]{0:T(512)} %fusion.31) | copy-start | bytes 6148
  246.1 12.9 %copy-start.34 = (bf16[512,4608]{1,0:T(8,128)(2,1)}, bf16[512,4608]{1,0:T(8,128)(2,1)S(1)}, u32[]{:S(2)}) copy-start(bf16[512,4608]{1,0:T(8,128)(2,1)S(1)} %get-tuple-element.105) | copy-start | bytes 14155780
  246.2 12.9 %copy-start.20 = (f32[512]{0:T(512)S(1)}, f32[512]{0:T(512)}, u32[]{:S(2)}) copy-start(f32[512]{0:T(512)} %copy-done.19) | copy-start | bytes 6148
  259.0 2.6 copy-start.32
  259.0 2.6 copy-start.3
  259.0 2.7 copy-start.5
  259.1 3.4 copy-start.6
  259.1 3.4 copy-start.12
  259.1 3.4 copy-start.13
  261.6 3.5 copy-start.21
  393.1 4.0 copy-start
  397.0 3.0 copy-start.15
  397.0 3.6 copy-start.14
  397.0 4.2 copy-start.29
  397.1 4.8 copy-start.28
  397.1 4.1 copy-start.16
  470.6 3.9 copy-start.33
  671.9 3.0 copy-start.4
  674.9 2.3 copy-start.27
  674.9 49.6 %copy-start.9 = (bf16[144,288]{1,0:T(8,128)(2,1)S(1)}, bf16[144,288]{1,0:T(8,128)(2,1)}, u32[]{:S(2)}) copy-start(bf16[144,288]{1,0:T(8,128)(2,1)} %param.20) | copy-start | bytes 248836
  674.9 49.6 %copy-start.10 = (bf16[144,288]{1,0:T(8,128)(2,1)S(1)}, bf16[144,288]{1,0:T(8,128)(2,1)}, u32[]{:S(2)}) copy-start(bf16[144,288]{1,0:T(8,128)(2,1)} %param.21) | copy-start | bytes 248836
  674.9 50.3 %copy-start.24 = (f32[288]{0:T(512)S(1)}, f32[288]{0:T(512)}, u32[]{:S(2)}) copy-start(f32[288]{0:T(512)} %param.27) | copy-start | bytes 3460
  674.9 50.9 %copy-start.7 = (bf16[2,256,1152]{2,1,0:T(8,128)(2,1)S(1)}, bf16[2,256,1152]{2,1,0:T(8,128)(2,1)}, u32[]{:S(2)}) copy-start(bf16[2,256,1152]{2,1,0:T(8,128)(2,1)} %get-tuple-element.127) | copy-start | bytes 3538948
  (3 other events, 3.2 us)
